TPU v7x, 32 devices: a whole 2x2x4 slice. The times are simulated.
32 devices in a mesh: sample: 4 (over z), gx: 2 (over core), gy: 2 (over x), gz: 2 (over y).
Axes of the slice: x: 2, y: 2, z: 4, core: 2. Of those that a mesh axis runs over, the one named last changes fastest.
Arguments:
- volume: bfloat16 [16, 32, 32, 128], P(('sample', 'gx'), 'gy', 'gz'), parts along dimension 0, may hold values from -6 to 6
- conv4_weight: bfloat16 [3, 3, 3, 128, 256], replicated, may hold values from -0.109375 to 0.109375
- conv5_weight: bfloat16 [3, 3, 3, 256, 512], P(None, None, None, None, ('gy', 'gz')), may hold values from -0.078125 to 0.078125
Outputs:
- features: bfloat16 [8, 16, 16, 512], P(('sample', 'gx'), None, None, ('gy', 'gz')), parts along dimension 0
There are 4 independent parts, one for each index of `sample`. A program takes and returns all parts, laid end to end along the dimension named above; an argument that names none is the same for every part. Nothing has to cross between parts.
All inputs are finite; a program needn't handle non-finite values.
Results may differ from a plain program's by a relative error of at most 0.009.
Values may be sent and summed in bfloat16 or wider, within the bound.
No kernel may reach another device: no remote copies, remote signals or barrier semaphores. Data moves between devices by JAX's collectives and lax.ppermute only.
A program may use at most 64 MiB of HBM per device.

v0:
```python
import jax
import jax.numpy as jnp
from jax import lax
from jax.sharding import PartitionSpec as P


def extended(cells, sides, width):
    for axis, dim in sides:
        count = lax.axis_size(axis)
        ends = count - 1
        head = lax.slice_in_dim(cells, 0, width, axis=dim)
        tail = lax.slice_in_dim(cells, cells.shape[dim] - width, cells.shape[dim], axis=dim)
        cells = jnp.concatenate(
            [
                lax.ppermute(tail, axis, [(i, (i + 1) % count) for i in range(ends)]),
                cells,
                lax.ppermute(head, axis, [((i + 1) % count, i) for i in range(ends)]),
            ],
            axis=dim,
        )
    return cells


def conv_local(padded, kernel):
    extent_x = padded.shape[0] - 2
    extent_y = padded.shape[1] - 2
    extent_z = padded.shape[2] - 2
    inputs = padded.shape[3]
    summed = None
    for along_x in range(3):
        for along_y in range(3):
            for along_z in range(3):
                window = padded[
                    along_x : along_x + extent_x,
                    along_y : along_y + extent_y,
                    along_z : along_z + extent_z,
                ]
                window = window.reshape(extent_x * extent_y * extent_z, inputs)
                contrib = jnp.dot(
                    window, kernel[along_x, along_y, along_z], preferred_element_type=jnp.float32
                )
                summed = contrib if summed is None else summed + contrib
    return summed.reshape(extent_x, extent_y, extent_z, kernel.shape[4])


def pool_leaky(hidden):
    leaked = jnp.where(hidden > 0, hidden, 0.3 * hidden)
    sizes = leaked.shape
    blocks = leaked.reshape(sizes[0] // 2, 2, sizes[1] // 2, 2, sizes[2] // 2, 2, sizes[3])
    return jnp.max(blocks, axis=(1, 3, 5)).astype(jnp.bfloat16)


def body(volume, conv4_weight, conv5_weight):
    padded = extended(volume, (("gx", 0), ("gy", 1), ("gz", 2)), 1)
    pooled = pool_leaky(conv_local(padded, conv4_weight))
    strips = lax.all_gather(pooled, "gz", axis=2, tiled=True)
    slab = lax.all_gather(strips, "gy", axis=1, tiled=True)
    bordered = extended(slab, (("gx", 0),), 1)
    bordered = jnp.pad(bordered, ((0, 0), (1, 1), (1, 1), (0, 0)))
    return conv_local(bordered, conv5_weight).astype(jnp.bfloat16)


def solution(mesh):
    return jax.shard_map(
        body,
        mesh=mesh,
        in_specs=(
            P(("sample", "gx"), "gy", "gz", None),
            P(),
            P(None, None, None, None, ("gy", "gz")),
        ),
        out_specs=P(("sample", "gx"), None, None, ("gy", "gz")),
        check_vma=False,
    )
```

profile of v0, /device:TPU:0, one launch (start us, length us, event | category | flops | bytes accessed | tf_op | source)
XLA Modules:
  0.0 55.4 jit_solution(4513016604005346935)
XLA Ops:
  0.0 1.0 %fusion.139 = (bf16[1,16,16,128]{3,2,1,0:T(8,128)(2,1)S(1)}, bf16[1,16,16,128]{3,2,1,0:T(8,128)(2,1)S(1)}) fusion(bf16[2,16,16,128]{3,2,1,0:T(8,128)(2,1)} %param.3), kind=kLoop, calls=%fused_computation.212 | loop fusion | bytes 262144 | tf_op jit(solution)/shard_map/slice | solution.py:11
  1.0 2.4 %collective-permute-start = (bf16[1,16,16,128]{3,2,1,0:T(8,128)(2,1)S(1)}, bf16[1,16,16,128]{3,2,1,0:T(8,128)(2,1)S(1)}, u32[]{:S(2)}, u32[]{:S(2)}) collective-permute-start(bf16[1,16,16,128]{3,2,1,0:T(8,128)(2,1)S(1)} %get-tuple-element.66), channel_id=1, source_target_pairs={{0,4},{1,5},{2,6},{3,7},{8,12},{9,13},{10,14},{11,15},{16,20},{17,... | collective-permute-start | bytes 196616 | tf_op jit(solution)/shard_map/ppermute | solution.py:15
  3.4 1.3 %collective-permute-start.1 = (bf16[1,16,16,128]{3,2,1,0:T(8,128)(2,1)S(1)}, bf16[1,16,16,128]{3,2,1,0:T(8,128)(2,1)S(1)}, u32[]{:S(2)}, u32[]{:S(2)}) collective-permute-start(bf16[1,16,16,128]{3,2,1,0:T(8,128)(2,1)S(1)} %get-tuple-element.65), channel_id=1, source_target_pairs={{4,0},{5,1},{6,2},{7,3},{12,8},{13,9},{14,10},{15,11},{20,16},{21,... | collective-permute-start | bytes 196616 | tf_op jit(solution)/shard_map/ppermute | solution.py:17
  4.7 1.8 %collective-permute-done.1 = bf16[1,16,16,128]{3,2,1,0:T(8,128)(2,1)S(1)} collective-permute-done((bf16[1,16,16,128]{3,2,1,0:T(8,128)(2,1)S(1)}, bf16[1,16,16,128]{3,2,1,0:T(8,128)(2,1)S(1)}, u32[]{:S(2)}, u32[]{:S(2)}) %collective-permute-start.1) | collective-permute-done | bytes 65568 | tf_op jit(solution)/shard_map/ppermute | solution.py:17
  6.5 1.0 %pad_maximum_fusion.2 = (bf16[2,16,16,128]{3,2,1,0:T(8,128)(2,1)S(1)}, bf16[4,16,16,128]{3,2,1,0:T(8,128)(2,1)S(1)}, bf16[2,16,16,128]{3,2,1,0:T(8,128)(2,1)S(1)}) fusion(bf16[1,16,16,128]{3,2,1,0:T(8,128)(2,1)S(1)} %collective-permute-done.1, bf16[2,16,16,128]{3,2,1,0:T(8,128)(2,1)} %param.3, ...), kind=kLoop, calls=%fused_computation.82 | loop fusion | flops 524288 | bytes 655360 | tf_op jit(solution)/shard_map/concatenate | solution.py:13
  7.6 4.2 %collective-permute-start.2 = (bf16[4,1,16,128]{3,2,1,0:T(8,128)(2,1)S(1)}, bf16[4,1,16,128]{3,2,1,0:T(8,128)(2,1)S(1)}, u32[]{:S(2)}, u32[]{:S(2)}) collective-permute-start(bf16[4,1,16,128]{3,2,1,0:T(8,128)(2,1)S(1)} %get-tuple-element.60), channel_id=1, source_target_pairs={{0,2},{1,3},{4,6},{5,7},{8,10},{9,11},{12,14},{13,15},{16,18},{17,... | collective-permute-start | bytes 49160 | tf_op jit(solution)/shard_map/ppermute | solution.py:15
  11.8 1.3 %collective-permute-start.3 = (bf16[4,1,16,128]{3,2,1,0:T(8,128)(2,1)S(1)}, bf16[4,1,16,128]{3,2,1,0:T(8,128)(2,1)S(1)}, u32[]{:S(2)}, u32[]{:S(2)}) collective-permute-start(bf16[4,1,16,128]{3,2,1,0:T(8,128)(2,1)S(1)} %get-tuple-element.61), channel_id=1, source_target_pairs={{2,0},{3,1},{6,4},{7,5},{10,8},{11,9},{14,12},{15,13},{18,16},{19,... | collective-permute-start | bytes 49160 | tf_op jit(solution)/shard_map/ppermute | solution.py:17
  13.2 4.2 %collective-permute-done.3 = bf16[4,1,16,128]{3,2,1,0:T(8,128)(2,1)S(1)} collective-permute-done((bf16[4,1,16,128]{3,2,1,0:T(8,128)(2,1)S(1)}, bf16[4,1,16,128]{3,2,1,0:T(8,128)(2,1)S(1)}, u32[]{:S(2)}, u32[]{:S(2)}) %collective-permute-start.3) | collective-permute-done | bytes 16416 | tf_op jit(solution)/shard_map/ppermute | solution.py:17
  17.5 3.4 %collective-permute-start.4 = (bf16[4,18,1,128]{3,2,1,0:T(2,128)(2,1)S(1)}, bf16[4,18,1,128]{3,2,1,0:T(2,128)(2,1)S(1)}, u32[]{:S(2)}, u32[]{:S(2)}) collective-permute-start(bf16[4,18,1,128]{3,2,1,0:T(2,128)(2,1)S(1)} %get-tuple-element.49), channel_id=1, source_target_pairs={{0,1},{2,3},{4,5},{6,7},{8,9},{10,11},{12,13},{14,15},{16,17},{18,... | collective-permute-start | bytes 55304 | tf_op jit(solution)/shard_map/ppermute | solution.py:15
  21.0 1.3 %collective-permute-start.5 = (bf16[4,18,1,128]{3,2,1,0:T(2,128)(2,1)S(1)}, bf16[4,18,1,128]{3,2,1,0:T(2,128)(2,1)S(1)}, u32[]{:S(2)}, u32[]{:S(2)}) collective-permute-start(bf16[4,18,1,128]{3,2,1,0:T(2,128)(2,1)S(1)} %get-tuple-element.50), channel_id=1, source_target_pairs={{1,0},{3,2},{5,4},{7,6},{9,8},{11,10},{13,12},{15,14},{17,16},{19,... | collective-permute-start | bytes 55304 | tf_op jit(solution)/shard_map/ppermute | solution.py:17
  22.3 0.2 fusion.77
  22.6 4.2 %collective-permute-done.5 = bf16[4,18,1,128]{3,2,1,0:T(2,128)(2,1)S(1)} collective-permute-done((bf16[4,18,1,128]{3,2,1,0:T(2,128)(2,1)S(1)}, bf16[4,18,1,128]{3,2,1,0:T(2,128)(2,1)S(1)}, u32[]{:S(2)}, u32[]{:S(2)}) %collective-permute-start.5) | collective-permute-done | bytes 18464 | tf_op jit(solution)/shard_map/ppermute | solution.py:17
  26.8 0.3 maximum_maximum_fusion
  27.1 0.3 fusion.136
  27.5 0.2 fusion.72
  28.3 0.2 convolution_add_fusion.21
  28.5 0.2 convolution_add_fusion.20
  28.7 0.2 convolution_add_fusion.19
  29.0 0.2 fusion.3
  29.2 0.2 convolution_add_fusion.17
  29.4 0.2 convolution_add_fusion.16
  29.6 0.2 convolution_add_fusion.15
  29.8 0.2 convolution_add_fusion.14
  30.0 0.2 convolution_add_fusion.13
  30.3 0.2 convolution_add_fusion.12
  30.5 0.2 convolution_add_fusion.11
  30.7 0.2 copy-done.2
  31.1 0.2 convolution_add_fusion.9
  31.4 0.2 convolution_add_fusion.8
  31.6 0.2 convolution_add_fusion.7
  31.8 0.2 convolution_add_fusion.6
  32.0 0.2 convolution_add_fusion.5
  32.2 0.2 fusion.4
  32.4 0.2 convolution_add_fusion.3
  32.7 0.2 fusion.5
  32.9 0.2 convolution_add_fusion.1
  33.1 0.2 fusion.6
  33.3 0.3 reshape.245
  33.6 0.5 fusion.13
  34.1 4.6 %all-gather = bf16[8,16,256]{2,1,0:T(8,128)(2,1)S(1)} all-gather(bf16[8,8,256]{2,1,0:T(8,128)(2,1)S(1)} %fusion.13), channel_id=2, replica_groups=mesh['sample'=4,'gx'=2,'gy'=2,'gz'=2] {'gz'}, dimensions={1}, use_global_device_ids=true | all-gather | bytes 98304 | tf_op jit(solution)/shard_map/all_gather | solution.py:56
  38.7 4.9 %all-gather.1 = bf16[16,16,256]{2,1,0:T(8,128)(2,1)S(1)} all-gather(bf16[8,16,256]{2,1,0:T(8,128)(2,1)S(1)} %all-gather), channel_id=3, replica_groups=mesh['sample'=4,'gx'=2,'gy'=2,'gz'=2] {'gy'}, dimensions={0}, use_global_device_ids=true | all-gather | bytes 196608 | tf_op jit(solution)/shard_map/all_gather | solution.py:57
  43.6 1.3 %collective-permute-start.6 = (bf16[1,16,16,256]{3,2,1,0:T(8,128)(2,1)S(1)}, bf16[1,16,16,256]{3,2,1,0:T(8,128)(2,1)S(1)}, u32[]{:S(2)}, u32[]{:S(2)}) collective-permute-start(bf16[1,16,16,256]{3,2,1,0:T(8,128)(2,1)S(1)} %bitcast.273), channel_id=1, source_target_pairs={{0,4},{1,5},{2,6},{3,7},{8,12},{9,13},{10,14},{11,15},{16,20},{17,... | collective-permute-start | bytes 393224 | tf_op jit(solution)/shard_map/ppermute | solution.py:15
  44.9 1.3 %collective-permute-start.7 = (bf16[1,16,16,256]{3,2,1,0:T(8,128)(2,1)S(1)}, bf16[1,16,16,256]{3,2,1,0:T(8,128)(2,1)S(1)}, u32[]{:S(2)}, u32[]{:S(2)}) collective-permute-start(bf16[1,16,16,256]{3,2,1,0:T(8,128)(2,1)S(1)} %bitcast.274), channel_id=1, source_target_pairs={{4,0},{5,1},{6,2},{7,3},{12,8},{13,9},{14,10},{15,11},{20,16},{21,... | collective-permute-start | bytes 393224 | tf_op jit(solution)/shard_map/ppermute | solution.py:17
  46.2 1.9 %collective-permute-done.7 = bf16[1,16,16,256]{3,2,1,0:T(8,128)(2,1)S(1)} collective-permute-done((bf16[1,16,16,256]{3,2,1,0:T(8,128)(2,1)S(1)}, bf16[1,16,16,256]{3,2,1,0:T(8,128)(2,1)S(1)}, u32[]{:S(2)}, u32[]{:S(2)}) %collective-permute-start.7) | collective-permute-done | bytes 131104 | tf_op jit(solution)/shard_map/ppermute | solution.py:17
  48.1 0.3 select_maximum_fusion
  48.5 0.3 fusion.134
  48.8 1.2 %copy-done.1 = bf16[3,3,3,256,128]{4,3,2,1,0:T(8,128)(2,1)S(1)} copy-done((bf16[3,3,3,256,128]{4,3,2,1,0:T(8,128)(2,1)S(1)}, bf16[3,3,3,256,128]{4,3,2,1,0:T(8,128)(2,1)}, u32[]{:S(2)}) %copy-start.1) | copy-done | bytes 1769496
  54.6 0.8 %fusion.9 = bf16[256,128]{1,0:T(8,128)(2,1)} fusion(f32[256,128]{1,0:T(8,128)S(1)} %convolution_add_fusion.23, bf16[256,256]{1,0:T(8,128)(2,1)S(1)} %bitcast.282, bf16[3,3,3,256,128]{4,3,2,1,0:T(8,128)(2,1)S(1)} %copy-done.1), kind=kOutput, calls=%fused_computation.60 | convolution fusion | flops 16842752 | bytes 393216 | tf_op jit(solution)/shard_map/dot_general | solution.py:39
  (44 shorter events, 5.6 us)
Async XLA Ops:
  0.0 22.3 %copy-start = (bf16[3,3,3,128,256]{4,3,2,1,0:T(8,128)(2,1)S(1)}, bf16[3,3,3,128,256]{4,3,2,1,0:T(8,128)(2,1)}, u32[]{:S(2)}) copy-start(bf16[3,3,3,128,256]{4,3,2,1,0:T(8,128)(2,1)} %param.4) | copy-start | bytes 5308420
  1.0 3.7 %collective-permute-start = (bf16[1,16,16,128]{3,2,1,0:T(8,128)(2,1)S(1)}, bf16[1,16,16,128]{3,2,1,0:T(8,128)(2,1)S(1)}, u32[]{:S(2)}, u32[]{:S(2)}) collective-permute-start(bf16[1,16,16,128]{3,2,1,0:T(8,128)(2,1)S(1)} %get-tuple-element.66), channel_id=1, source_target_pairs={{0,4},{1,5},{2,6},{3,7},{8,12},{9,13},{10,14},{11,15},{16,20},{17,... | collective-permute-start | bytes 196616 | tf_op jit(solution)/shard_map/ppermute | solution.py:15
  3.4 3.1 %collective-permute-start.1 = (bf16[1,16,16,128]{3,2,1,0:T(8,128)(2,1)S(1)}, bf16[1,16,16,128]{3,2,1,0:T(8,128)(2,1)S(1)}, u32[]{:S(2)}, u32[]{:S(2)}) collective-permute-start(bf16[1,16,16,128]{3,2,1,0:T(8,128)(2,1)S(1)} %get-tuple-element.65), channel_id=1, source_target_pairs={{4,0},{5,1},{6,2},{7,3},{12,8},{13,9},{14,10},{15,11},{20,16},{21,... | collective-permute-start | bytes 196616 | tf_op jit(solution)/shard_map/ppermute | solution.py:17
  7.6 5.7 %collective-permute-start.2 = (bf16[4,1,16,128]{3,2,1,0:T(8,128)(2,1)S(1)}, bf16[4,1,16,128]{3,2,1,0:T(8,128)(2,1)S(1)}, u32[]{:S(2)}, u32[]{:S(2)}) collective-permute-start(bf16[4,1,16,128]{3,2,1,0:T(8,128)(2,1)S(1)} %get-tuple-element.60), channel_id=1, source_target_pairs={{0,2},{1,3},{4,6},{5,7},{8,10},{9,11},{12,14},{13,15},{16,18},{17,... | collective-permute-start | bytes 49160 | tf_op jit(solution)/shard_map/ppermute | solution.py:15
  11.8 5.6 %collective-permute-start.3 = (bf16[4,1,16,128]{3,2,1,0:T(8,128)(2,1)S(1)}, bf16[4,1,16,128]{3,2,1,0:T(8,128)(2,1)S(1)}, u32[]{:S(2)}, u32[]{:S(2)}) collective-permute-start(bf16[4,1,16,128]{3,2,1,0:T(8,128)(2,1)S(1)} %get-tuple-element.61), channel_id=1, source_target_pairs={{2,0},{3,1},{6,4},{7,5},{10,8},{11,9},{14,12},{15,13},{18,16},{19,... | collective-permute-start | bytes 49160 | tf_op jit(solution)/shard_map/ppermute | solution.py:17
  17.5 5.0 %collective-permute-start.4 = (bf16[4,18,1,128]{3,2,1,0:T(2,128)(2,1)S(1)}, bf16[4,18,1,128]{3,2,1,0:T(2,128)(2,1)S(1)}, u32[]{:S(2)}, u32[]{:S(2)}) collective-permute-start(bf16[4,18,1,128]{3,2,1,0:T(2,128)(2,1)S(1)} %get-tuple-element.49), channel_id=1, source_target_pairs={{0,1},{2,3},{4,5},{6,7},{8,9},{10,11},{12,13},{14,15},{16,17},{18,... | collective-permute-start | bytes 55304 | tf_op jit(solution)/shard_map/ppermute | solution.py:15
  21.0 5.9 %collective-permute-start.5 = (bf16[4,18,1,128]{3,2,1,0:T(2,128)(2,1)S(1)}, bf16[4,18,1,128]{3,2,1,0:T(2,128)(2,1)S(1)}, u32[]{:S(2)}, u32[]{:S(2)}) collective-permute-start(bf16[4,18,1,128]{3,2,1,0:T(2,128)(2,1)S(1)} %get-tuple-element.50), channel_id=1, source_target_pairs={{1,0},{3,2},{5,4},{7,6},{9,8},{11,10},{13,12},{15,14},{17,16},{19,... | collective-permute-start | bytes 55304 | tf_op jit(solution)/shard_map/ppermute | solution.py:17
  30.0 0.9 %copy-start.2 = (bf16[2,16,16,128]{3,2,1,0:T(8,128)(2,1)S(1)}, bf16[2,16,16,128]{3,2,1,0:T(8,128)(2,1)}, u32[]{:S(2)}) copy-start(bf16[2,16,16,128]{3,2,1,0:T(8,128)(2,1)} %param.3) | copy-start | bytes 393220
  43.6 2.6 %collective-permute-start.6 = (bf16[1,16,16,256]{3,2,1,0:T(8,128)(2,1)S(1)}, bf16[1,16,16,256]{3,2,1,0:T(8,128)(2,1)S(1)}, u32[]{:S(2)}, u32[]{:S(2)}) collective-permute-start(bf16[1,16,16,256]{3,2,1,0:T(8,128)(2,1)S(1)} %bitcast.273), channel_id=1, source_target_pairs={{0,4},{1,5},{2,6},{3,7},{8,12},{9,13},{10,14},{11,15},{16,20},{17,... | collective-permute-start | bytes 393224 | tf_op jit(solution)/shard_map/ppermute | solution.py:15
  44.9 3.2 %collective-permute-start.7 = (bf16[1,16,16,256]{3,2,1,0:T(8,128)(2,1)S(1)}, bf16[1,16,16,256]{3,2,1,0:T(8,128)(2,1)S(1)}, u32[]{:S(2)}, u32[]{:S(2)}) collective-permute-start(bf16[1,16,16,256]{3,2,1,0:T(8,128)(2,1)S(1)} %bitcast.274), channel_id=1, source_target_pairs={{4,0},{5,1},{6,2},{7,3},{12,8},{13,9},{14,10},{15,11},{20,16},{21,... | collective-permute-start | bytes 393224 | tf_op jit(solution)/shard_map/ppermute | solution.py:17
  48.5 1.5 %copy-start.1 = (bf16[3,3,3,256,128]{4,3,2,1,0:T(8,128)(2,1)S(1)}, bf16[3,3,3,256,128]{4,3,2,1,0:T(8,128)(2,1)}, u32[]{:S(2)}) copy-start(bf16[3,3,3,256,128]{4,3,2,1,0:T(8,128)(2,1)} %param.5) | copy-start | bytes 5308420
where the time goes:
time: 55.7 us; the launch traced here: 55.4 us
  starting transfers between devices  16.5 us (30%)
  waiting for transfers between devices  12.4 us (22%)
  matrix products  10.8 us (19%)
  blocking collectives  9.52 us (17%)
  local copies, waits for them, and re-layouts  3.45 us (6%)
  other arithmetic  2.17 us (4%)
  between operations  0.57 us (1%)
    ppermute x4, waiting for transfers between devices, extended(): lax.ppermute(head, axis, [((i + 1) % count, i) for i in range(ends)])  12.2 us
    ppermute x4, starting transfers between devices, extended(): lax.ppermute(tail, axis, [(i, (i + 1) % count) for i in range(ends)])  11.3 us
    dot_general x54, matrix products, conv_local(): jnp.dot(window, kernel[along_x, along_y, along_z], preferred_element_type...  10.8 us
    ppermute x4, starting transfers between devices, extended(): lax.ppermute(head, axis, [((i + 1) % count, i) for i in range(ends)])  5.17 us
    all_gather x1, blocking collectives, body(): slab = lax.all_gather(strips, 'gy', axis=1, tiled=True)  4.93 us
    all_gather x1, blocking collectives, body(): strips = lax.all_gather(pooled, 'gz', axis=2, tiled=True)  4.59 us
    concatenate x4, other arithmetic, extended(): jnp.concatenate([lax.ppermute(tail, axis, [(i, (i + 1) % count) for i in...  1.66 us
    unnamed x7, local copies, waits for them, and re-layouts  1.41 us
  transfers between devices with their start and end apart: 8, of which 5 were waited for; matrix products, arithmetic and copies ran while one was open for 0% of the time, Pallas kernels for 0%

commit v1 on v0

--- a/solution.py
+++ b/solution.py
@@ -1,7 +1,17 @@
+import functools
+
 import jax
 import jax.numpy as jnp
 from jax import lax
+from jax.experimental import pallas as pl
+from jax.experimental.pallas import tpu as pltpu
 from jax.sharding import PartitionSpec as P
+
+BF = jnp.bfloat16
+F32 = jnp.float32
+VMEM = pl.BlockSpec(memory_space=pltpu.VMEM)
+SMEM = pl.BlockSpec(memory_space=pltpu.SMEM)
+GROUP = ("gx", "gy", "gz")
 
 
 def extended(cells, sides, width):
@@ -50,7 +60,7 @@
     return jnp.max(blocks, axis=(1, 3, 5)).astype(jnp.bfloat16)
 
 
-def body(volume, conv4_weight, conv5_weight):
+def general_body(volume, conv4_weight, conv5_weight):
     padded = extended(volume, (("gx", 0), ("gy", 1), ("gz", 2)), 1)
     pooled = pool_leaky(conv_local(padded, conv4_weight))
     strips = lax.all_gather(pooled, "gz", axis=2, tiled=True)
@@ -58,6 +68,285 @@
     bordered = extended(slab, (("gx", 0),), 1)
     bordered = jnp.pad(bordered, ((0, 0), (1, 1), (1, 1), (0, 0)))
     return conv_local(bordered, conv5_weight).astype(jnp.bfloat16)
+
+
+def leaky(v):
+    return jnp.where(v > 0, v, 0.3 * v)
+
+
+def shifted_copies(plane, out_ref, index):
+    ny, nz, nc = plane.shape
+    flat = plane.reshape(ny * nz, nc).astype(F32)
+    at = lax.broadcasted_iota(jnp.int32, flat.shape, 0) % nz
+    after = jnp.where(at == 0, 0.0, pltpu.roll(flat, 1, 0))
+    before = jnp.where(at == nz - 1, 0.0, pltpu.roll(flat, ny * nz - 1, 0))
+    none = jnp.zeros((2, nz, nc), BF)
+    for dz, moved in enumerate((after, flat, before)):
+        out_ref[dz, index, 0:2] = none
+        out_ref[dz, index, 2 + ny : 4 + ny] = none
+        out_ref[dz, index, 2 : 2 + ny] = moved.astype(BF).reshape(ny, nz, nc)
+
+
+def windows(shift_ref, index, first, ny):
+    nz, nc = shift_ref.shape[3:]
+    parts = []
+    for dy in range(3):
+        for dz in range(3):
+            part = shift_ref[dz, index, pl.ds(first + dy, ny + 1)]
+            parts.append(part.reshape((ny + 1) * nz, nc))
+    return jnp.concatenate(parts, axis=1)
+
+
+def edge_windows(plane, flat_ref, col_ref, index, at_y, at_z):
+    ny, nz, nc = plane.shape
+    flat_ref[index] = plane.reshape(ny * nz, nc).astype(F32)
+    low = flat_ref[index, pl.ds(0, ny, nz), :]
+    high = flat_ref[index, pl.ds(nz - 1, ny, nz), :]
+    col_ref[index] = jnp.zeros(col_ref.shape[1:], F32)
+    col_ref[index, 8 : 8 + ny] = jnp.where(at_z == 0, high, low)
+    parts = []
+    for dy in range(3):
+        near = col_ref[index, 7 + dy : 15 + dy + ny]
+        far = col_ref[index, 6 + dy : 14 + dy + ny]
+        parts.append(jnp.where(at_y == 0, near, far).astype(BF))
+    return jnp.concatenate(parts, axis=1)
+
+
+def edge_weights(w_ref, dx, at_z):
+    taps = w_ref.shape[1]
+    return jnp.concatenate([w_ref[dx, dy, 2 * at_z] for dy in range(taps)], axis=0)
+
+
+def own_kernel(at_ref, v_ref, w_ref, h_ref, t_ref, shift_ref, flat_ref, col_ref):
+    at_y, at_z = at_ref[1], at_ref[2]
+    planes, ny, nz, nc = v_ref.shape
+    filters = w_ref.shape[4]
+    for p in range(planes):
+        shifted_copies(v_ref[p], shift_ref, p)
+    wins = [windows(shift_ref, p, 1 - at_y, ny) for p in range(planes)]
+    for p in range(planes):
+        lhs = jnp.concatenate(wins, axis=1)
+        rhs = w_ref[1 - p : 3 - p].reshape(2 * 9 * nc, filters)
+        h_ref[p] = jnp.dot(lhs, rhs, preferred_element_type=F32).reshape(h_ref.shape[1:])
+    edges = [edge_windows(v_ref[p], flat_ref, col_ref, p, at_y, at_z) for p in range(planes)]
+    lhs = jnp.concatenate(edges, axis=1)
+    for p in range(planes):
+        rhs = jnp.concatenate([edge_weights(w_ref, 1 - p, at_z), edge_weights(w_ref, 2 - p, at_z)], axis=0)
+        t_ref[p] = jnp.dot(lhs, rhs, preferred_element_type=F32)
+
+
+def put(out_ref, first, rows):
+    out_ref[first : first + rows.shape[0]] = rows.astype(out_ref.dtype)
+
+
+def pack_kernel(at_ref, r_ref, w_ref, h_in, t_in, out_ref, h_ref, t_ref, shift_ref, flat_ref, col_ref, pair_ref):
+    at_x, at_y, at_z = at_ref[0], at_ref[1], at_ref[2]
+    planes, ny, nz, nc = r_ref.shape
+    filters = w_ref.shape[4]
+    plane = r_ref[at_x]
+    dx, mine = 2 * (1 - at_x), 1 - at_x
+    shifted_copies(plane, shift_ref, 0)
+    lhs = windows(shift_ref, 0, 1 - at_y, ny)
+    rhs = w_ref[dx].reshape(9 * nc, filters)
+    for p in range(planes):
+        h_ref[p * (ny + 1) * nz : (p + 1) * (ny + 1) * nz] = h_in[p].reshape((ny + 1) * nz, filters)
+    begin = pl.multiple_of(mine * (ny + 1) * nz, 8)
+    h_ref[pl.ds(begin, (ny + 1) * nz)] += jnp.dot(lhs, rhs, preferred_element_type=F32)
+    edge = edge_windows(plane, flat_ref, col_ref, 0, at_y, at_z)
+    t_ref[...] = t_in[...]
+    t_ref[mine] += jnp.dot(edge, edge_weights(w_ref, dx, at_z), preferred_element_type=F32)
+
+    def row(p, e):
+        return h_ref[pl.ds(pl.multiple_of((p * (ny + 1) + e) * nz, 8), nz)]
+
+    low = -jnp.inf
+    is_edge = lax.broadcasted_iota(jnp.int32, (nz, filters), 0) == (nz - 1) * (1 - at_z)
+    for k in range(ny // 2):
+        first = jnp.maximum(row(0, at_y + 2 * k), row(1, at_y + 2 * k))
+        second = jnp.maximum(row(0, at_y + 2 * k + 1), row(1, at_y + 2 * k + 1))
+        if k == 0:
+            first = jnp.where(at_y == 1, low, first)
+        if k == ny // 2 - 1:
+            second = jnp.where(at_y == 0, low, second)
+        both = jnp.where(is_edge, low, jnp.maximum(first, second))
+        for half in range(filters // 128):
+            pair_ref[half, k * nz : (k + 1) * nz] = both[:, half * 128 : (half + 1) * 128]
+    pooled = [
+        jnp.maximum(
+            pair_ref[half, pl.ds(0, ny * nz // 4, 2), :],
+            pair_ref[half, pl.ds(1, ny * nz // 4, 2), :],
+        )
+        for half in range(filters // 128)
+    ]
+    cells = ny * nz // 4
+    put(out_ref, 0, leaky(jnp.concatenate(pooled, axis=1)))
+    for p in range(planes):
+        put(out_ref, cells + p * nz, row(p, (ny - 1) * (1 - at_y) + at_y))
+        put(out_ref, cells + planes * nz + p * nz, row(p, ny * (1 - at_y)))
+        base = cells + 2 * planes * nz
+        here = p * (ny + 1) * nz
+        column = []
+        for half in range(filters // 128):
+            part = slice(half * 128, (half + 1) * 128)
+            flat = pair_ref.at[half]
+            for e in range(ny + 1):
+                flat[e * nz : (e + 1) * nz] = h_ref[here + e * nz : here + (e + 1) * nz, part]
+            picks = [flat[pl.ds(e * nz + z, ny, nz), :] for e in (0, 1) for z in (0, nz - 1)]
+            column.append(
+                jnp.where(
+                    at_y == 0,
+                    jnp.where(at_z == 0, picks[1], picks[0]),
+                    jnp.where(at_z == 0, picks[3], picks[2]),
+                )
+            )
+        put(out_ref, base + p * ny, jnp.concatenate(column, axis=1))
+        base += planes * ny
+        put(out_ref, base + p * ny, jnp.where(at_y == 0, t_ref[p, 0:ny], t_ref[p, 1 : ny + 1]))
+    base += planes * ny
+    corner = jnp.where(at_y == 0, t_ref[:, ny : ny + 1], t_ref[:, 0:1])
+    at = lax.broadcasted_iota(jnp.int32, (16, filters), 0)
+    put(out_ref, base, jnp.where(at == 0, corner[0], jnp.where(at == 1, corner[1], 0.0)))
+
+
+def finish_kernel(at_ref, q0, q1, q2, q3, w_ref, own_ref, other_ref, pack_ref, full_ref, pair_ref, shift_ref, *, ny, nz, planes):
+    at_x, at_y, at_z = at_ref[0], at_ref[1], at_ref[2]
+    filters = w_ref.shape[3]
+    outs = w_ref.shape[4]
+    here = 2 * at_y + at_z
+    pack_ref[here] = q0[...]
+    pack_ref[2 * (1 - at_y) + at_z] = q1[...]
+    pack_ref[2 * at_y + 1 - at_z] = q2[...]
+    pack_ref[2 * (1 - at_y) + 1 - at_z] = q3[...]
+    py, pz = ny // 2, nz // 2
+    cells = py * pz
+    row_at = cells
+    over_y = row_at + planes * nz
+    col_at = over_y + planes * nz
+    over_z = col_at + planes * ny
+    over_c = over_z + planes * ny
+
+    def take(q, first, count):
+        return pack_ref[q, first : first + count].astype(F32)
+
+    def halve(v, slot):
+        parts = []
+        for half in range(filters // 128):
+            pair_ref[slot, half] = v[:, half * 128 : (half + 1) * 128]
+            count = v.shape[0] // 2
+            parts.append(
+                jnp.maximum(pair_ref[slot, half, pl.ds(0, count, 2), :], pair_ref[slot, half, pl.ds(1, count, 2), :])
+            )
+        return jnp.concatenate(parts, axis=1)
+
+    for qy in range(2):
+        for qz in range(2):
+            q, by_y, by_z, by_both = 2 * qy + qz, 2 * (1 - qy) + qz, 2 * qy + 1 - qz, 2 * (1 - qy) + 1 - qz
+            y_edge, z_edge = (ny - 1) * (1 - qy), (nz - 1) * (1 - qz)
+            corner = take(by_both, over_c, 16)
+            edge_row, edge_col = None, None
+            at = lax.broadcasted_iota(jnp.int32, (nz, filters), 0)
+            for p in range(planes):
+                across = take(by_z, over_z + p * ny, ny)
+                extra = across[y_edge : y_edge + 1] + corner[p : p + 1]
+                line = take(q, row_at + p * nz, nz) + take(by_y, over_y + p * nz, nz)
+                line = jnp.where(at == z_edge, line + extra, line)
+                edge_row = line if edge_row is None else jnp.maximum(edge_row, line)
+                line = take(q, col_at + p * ny, ny) + across
+                edge_col = line if edge_col is None else jnp.maximum(edge_col, line)
+            edge_col = jnp.where(at == y_edge, -jnp.inf, edge_col)
+            edge_row = leaky(halve(edge_row, 0))
+            edge_col = leaky(halve(edge_col, 1))
+            pooled = take(q, 0, cells).reshape(py, pz, filters)
+            inner = lax.broadcasted_iota(jnp.int32, (py, pz, filters), 1) == (pz - 1) * (1 - qz)
+            pooled = jnp.where(inner, jnp.maximum(pooled, edge_col[:, None, :]), pooled)
+            inner = lax.broadcasted_iota(jnp.int32, (py, pz, filters), 0) == (py - 1) * (1 - qy)
+            pooled = jnp.where(inner, jnp.maximum(pooled, edge_row[None]), pooled)
+            full_ref[qy * py : (qy + 1) * py, qz * pz : (qz + 1) * pz] = pooled
+    shifted_copies(full_ref[...].astype(BF), shift_ref, 0)
+    parts = []
+    for dy in range(3):
+        for dz in range(3):
+            parts.append(shift_ref[dz, 0, 1 + dy : 1 + dy + ny].reshape(ny * nz, filters))
+    lhs = jnp.concatenate(parts, axis=1)
+    rhs = jnp.concatenate(
+        [w_ref[1].reshape(9 * filters, outs), w_ref[2 * at_x].reshape(9 * filters, outs)], axis=1
+    )
+    sums = jnp.dot(lhs, rhs, preferred_element_type=F32)
+    own_ref[...] = sums[:, :outs]
+    other_ref[...] = sums[:, outs:]
+
+
+def pair_body(volume, conv4_weight, conv5_weight):
+    planes, ny, nz, nc = volume.shape
+    f4, f5 = conv4_weight.shape[4], conv5_weight.shape[4]
+    at = jnp.stack([lax.axis_index(axis) for axis in GROUP]).astype(jnp.int32)
+
+    def swap(x, flips):
+        return lax.ppermute(x, GROUP, [(i, i ^ flips) for i in range(8)])
+
+    cost = functools.partial(pl.CostEstimate, transcendentals=0)
+    rows = (ny + 1) * nz
+    theirs = swap(volume, 4)
+    hidden, past = pl.pallas_call(
+        own_kernel,
+        out_shape=(
+            jax.ShapeDtypeStruct((planes, ny + 1, nz, f4), F32),
+            jax.ShapeDtypeStruct((planes, ny + 8, f4), F32),
+        ),
+        in_specs=[SMEM, VMEM, VMEM],
+        out_specs=(VMEM, VMEM),
+        scratch_shapes=[
+            pltpu.VMEM((3, planes, ny + 4, nz, nc), BF),
+            pltpu.VMEM((planes, ny * nz, nc), F32),
+            pltpu.VMEM((planes, ny + 24, nc), F32),
+        ],
+        cost_estimate=cost(flops=2 * planes * rows * 18 * nc * f4, bytes_accessed=54 * nc * f4),
+        name="own_planes",
+    )(at, volume, conv4_weight)
+    cells = ny * nz // 4
+    packed = cells + planes * (2 * nz + 2 * ny) + 16
+    pack = pl.pallas_call(
+        pack_kernel,
+        out_shape=jax.ShapeDtypeStruct((packed, f4), BF),
+        in_specs=[SMEM, VMEM, VMEM, VMEM, VMEM],
+        out_specs=VMEM,
+        scratch_shapes=[
+            pltpu.VMEM((planes * rows, f4), F32),
+            pltpu.VMEM((planes, ny + 8, f4), F32),
+            pltpu.VMEM((3, 1, ny + 4, nz, nc), BF),
+            pltpu.VMEM((1, ny * nz, nc), F32),
+            pltpu.VMEM((1, ny + 24, nc), F32),
+            pltpu.VMEM((f4 // 128, rows, 128), F32),
+        ],
+        cost_estimate=cost(flops=2 * rows * 9 * nc * f4, bytes_accessed=18 * nc * f4),
+        name="pool_and_pack",
+    )(at, theirs, conv4_weight, hidden, past)
+    by_y = swap(pack, 2)
+    by_z = swap(pack, 1)
+    by_both = swap(pack, 3)
+    gy, gz = 2 * ny // 2, 2 * nz // 2
+    own, other = pl.pallas_call(
+        functools.partial(finish_kernel, ny=ny, nz=nz, planes=planes),
+        out_shape=(jax.ShapeDtypeStruct((gy * gz, f5), F32), jax.ShapeDtypeStruct((gy * gz, f5), F32)),
+        in_specs=[SMEM] + [VMEM] * 5,
+        out_specs=(VMEM, VMEM),
+        scratch_shapes=[
+            pltpu.VMEM((4, packed, f4), BF),
+            pltpu.VMEM((gy, gz, f4), F32),
+            pltpu.VMEM((2, f4 // 128, max(ny, nz), 128), F32),
+            pltpu.VMEM((3, 1, gy + 4, gz, f4), BF),
+        ],
+        cost_estimate=cost(flops=4 * gy * gz * 9 * f4 * f5, bytes_accessed=36 * f4 * f5),
+        name="finish_and_conv5",
+    )(at, pack, by_y, by_z, by_both, conv5_weight)
+    features = (own + swap(other, 4)).astype(BF)
+    return features.reshape(1, gy, gz, f5)
+
+
+def body(volume, conv4_weight, conv5_weight):
+    if all(lax.axis_size(axis) == 2 for axis in GROUP) and volume.shape[0] == 2:
+        return pair_body(volume, conv4_weight, conv5_weight)
+    return general_body(volume, conv4_weight, conv5_weight)
 
 
 def solution(mesh):

time: 55.7 us -> 25.1 us (0.45)
  starting transfers between devices: 16.5 us -> 4.5 us
  matrix products: 10.8 us -> 0 us
  blocking collectives: 9.52 us -> 0 us
  Pallas kernels: 0 us -> 9.14 us
  waiting for transfers between devices: 12.4 us -> 7.35 us
  local copies, waits for them, and re-layouts: 3.45 us -> 1.64 us
    ppermute x8 -> x5, starting transfers between devices: 16.5 us -> 4.5 us  [swap(): return lax.ppermute(x, GROUP, [(i, i ^ flips) for i in range(8)])]
    dot_general x54 -> x0, matrix products: 10.8 us -> none  [conv_local(): jnp.dot(window, kernel[along_x, along_y, along_z], preferred_element_type...]
    all_gather x2 -> x0, blocking collectives: 9.52 us -> none  [the longest x1 4.93 us: body(): slab = lax.all_gather(strips, 'gy', axis=1, tiled=True)]
    pallas_call x0 -> x3, Pallas kernels: none -> 9.14 us  [the longest x1 3.34 us: pair_body(): pl.pallas_call(own_kernel, out_shape=(jax.ShapeDtypeStruct((planes, ny +...]
    ppermute x8 -> x5, waiting for transfers between devices: 12.4 us -> 7.35 us  [swap(): return lax.ppermute(x, GROUP, [(i, i ^ flips) for i in range(8)])]
    slice x5 -> x0, local copies, waits for them, and re-layouts: 1.72 us -> none  [the longest x1 1.01 us: extended(): head = lax.slice_in_dim(cells, 0, width, axis=dim)]
    concatenate x4 -> x0, other arithmetic: 1.66 us -> none  [extended(): jnp.concatenate([lax.ppermute(tail, axis, [(i, (i + 1) % count) for i in...]
    convert_element_type x0 -> x1, other arithmetic: none -> 1.56 us  [pair_body(): features = (own + swap(other, 4)).astype(BF)]
  transfers between devices with their start and end apart: 8 -> 5, of which waited for: 5 -> 4; matrix products, arithmetic and copies ran while one was open for 0% -> 3% of each run, Pallas kernels for 0% -> 13%
where the time goes in v1:
time: 25.1 us; the launch traced here: 24.9 us
  Pallas kernels  9.14 us (36%)
  waiting for transfers between devices  7.35 us (29%)
  starting transfers between devices  4.5 us (18%)
  other arithmetic  2.21 us (9%)
  local copies, waits for them, and re-layouts  1.64 us (7%)
    ppermute x5, waiting for transfers between devices, swap(): return lax.ppermute(x, GROUP, [(i, i ^ flips) for i in range(8)])  7.35 us
    ppermute x5, starting transfers between devices, swap(): return lax.ppermute(x, GROUP, [(i, i ^ flips) for i in range(8)])  4.5 us
    pallas_call x1, Pallas kernels, pair_body(): pl.pallas_call(own_kernel, out_shape=(jax.ShapeDtypeStruct((planes, ny +...  3.34 us
    pallas_call x1, Pallas kernels, pair_body(): pl.pallas_call(functools.partial(finish_kernel, ny=ny, nz=nz, planes=plan...  3 us
    pallas_call x1, Pallas kernels, pair_body(): pl.pallas_call(pack_kernel, out_shape=jax.ShapeDtypeStruct((packed, f4),...  2.8 us
    unnamed x8, local copies, waits for them, and re-layouts  1.64 us
    convert_element_type x1, other arithmetic, pair_body(): features = (own + swap(other, 4)).astype(BF)  1.56 us
    another operation x1, other arithmetic, pair_body(): at = jnp.stack([lax.axis_index(axis) for axis in GROUP]).astype(jnp.int32)  0.65 us
  transfers between devices with their start and end apart: 5, of which 4 were waited for; matrix products, arithmetic and copies ran while one was open for 3% of the time, Pallas kernels for 13%

profile of v1, /device:TPU:0, one launch (start us, length us, event | category | flops | bytes accessed | tf_op | source)
XLA Modules:
  0.0 24.9 jit_solution(13571033967469953944)
XLA Ops:
  0.0 0.5 %collective-permute-start = (bf16[2,16,16,128]{3,2,1,0:T(8,128)(2,1)}, bf16[2,16,16,128]{3,2,1,0:T(8,128)(2,1)S(1)}, u32[]{:S(2)}, u32[]{:S(2)}) collective-permute-start(bf16[2,16,16,128]{3,2,1,0:T(8,128)(2,1)} %v_ref.1), channel_id=1, source_target_pairs={{0,4},{1,5},{2,6},{3,7},{4,0},{5,1},{6,2},{7,3},{8,12},{9,13},{10,... | collective-permute-start | bytes 393224 | tf_op jit(solution)/shard_map/ppermute | solution.py:285
  0.5 0.7 %pad_add_fusion.at_ref = s32[3]{0:T(128)} fusion(s32[1]{0:T(128)} %bitcast.2, s32[1]{0:T(128)} %bitcast.1, s32[1]{0:T(128)} %bitcast), kind=kLoop, calls=%fused_computation.1 | loop fusion | flops 6 | bytes 24 | tf_op jit(solution)/shard_map/stack | solution.py:282
  1.1 3.3 %own_planes.1 = (f32[2,17,16,256]{3,2,1,0:T(8,128)}, f32[2,24,256]{2,1,0:T(8,128)}) custom-call(s32[3]{0:T(128)} %pad_add_fusion.at_ref, bf16[2,16,16,128]{3,2,1,0:T(8,128)(2,1)} %v_ref.1, bf16[3,3,3,128,256]{4,3,2,1,0:T(8,128)(2,1)} %w_ref.4), custom_call_target="tpu_custom_call" | custom-call | flops 641728512 | bytes 1769472 | tf_op jit(solution)/shard_map/own_planes/pallas_call | solution.py:290
  4.4 0.0 collective-permute-done.r_ref
  4.4 0.0 copy-start
  4.5 0.6 %copy-done = bf16[2,16,16,128]{3,2,1,0:T(8,128)(2,1)} copy-done((bf16[2,16,16,128]{3,2,1,0:T(8,128)(2,1)}, bf16[2,16,16,128]{3,2,1,0:T(8,128)(2,1)S(1)}, u32[]{:S(2)}) %copy-start) | copy-done | bytes 131096
  5.1 2.8 %pool_and_pack.1.q0 = bf16[208,256]{1,0:T(8,128)(2,1)} custom-call(s32[3]{0:T(128)} %pad_add_fusion.at_ref, bf16[2,16,16,128]{3,2,1,0:T(8,128)(2,1)} %copy-done, bf16[3,3,3,128,256]{4,3,2,1,0:T(8,128)(2,1)} %w_ref.4, f32[2,17,16,256]{3,2,1,0:T(8,128)} %get-tuple-element.9.h_in, f32[2,24,256]{2,1,0:T(8,128)} %get-tuple-element.10.t_in), custom_call_target="tpu_custom_call" | custom-call | flops 160432128 | bytes 589824 | tf_op jit(solution)/shard_map/pool_and_pack/pallas_call | solution.py:308
  7.9 3.4 %collective-permute-start.3 = (bf16[208,256]{1,0:T(8,128)(2,1)}, bf16[208,256]{1,0:T(8,128)(2,1)S(1)}, u32[]{:S(2)}, u32[]{:S(2)}) collective-permute-start(bf16[208,256]{1,0:T(8,128)(2,1)} %pool_and_pack.1.q0), channel_id=1, source_target_pairs={{0,3},{1,2},{2,1},{3,0},{4,7},{5,6},{6,5},{7,4},{8,11},{9,10},{10,... | collective-permute-start | bytes 319496 | tf_op jit(solution)/shard_map/ppermute | solution.py:285
  11.3 0.5 %collective-permute-start.2 = (bf16[208,256]{1,0:T(8,128)(2,1)}, bf16[208,256]{1,0:T(8,128)(2,1)S(1)}, u32[]{:S(2)}, u32[]{:S(2)}) collective-permute-start(bf16[208,256]{1,0:T(8,128)(2,1)} %pool_and_pack.1.q0), channel_id=1, source_target_pairs={{0,1},{1,0},{2,3},{3,2},{4,5},{5,4},{6,7},{7,6},{8,9},{9,8},{10,11... | collective-permute-start | bytes 319496 | tf_op jit(solution)/shard_map/ppermute | solution.py:285
  11.8 0.1 collective-permute-start.1
  11.9 3.4 %collective-permute-done.3.q3 = bf16[208,256]{1,0:T(8,128)(2,1)S(1)} collective-permute-done((bf16[208,256]{1,0:T(8,128)(2,1)}, bf16[208,256]{1,0:T(8,128)(2,1)S(1)}, u32[]{:S(2)}, u32[]{:S(2)}) %collective-permute-start.3) | collective-permute-done | bytes 106528 | tf_op jit(solution)/shard_map/ppermute | solution.py:285
  15.3 0.0 copy-start.1
  15.3 2.2 %collective-permute-done.2.q2 = bf16[208,256]{1,0:T(8,128)(2,1)S(1)} collective-permute-done((bf16[208,256]{1,0:T(8,128)(2,1)}, bf16[208,256]{1,0:T(8,128)(2,1)S(1)}, u32[]{:S(2)}, u32[]{:S(2)}) %collective-permute-start.2) | collective-permute-done | bytes 106528 | tf_op jit(solution)/shard_map/ppermute | solution.py:285
  17.5 0.0 copy-start.2
  17.5 0.3 %collective-permute-done.1.q1 = bf16[208,256]{1,0:T(8,128)(2,1)S(1)} collective-permute-done((bf16[208,256]{1,0:T(8,128)(2,1)}, bf16[208,256]{1,0:T(8,128)(2,1)S(1)}, u32[]{:S(2)}, u32[]{:S(2)}) %collective-permute-start.1) | collective-permute-done | bytes 106528 | tf_op jit(solution)/shard_map/ppermute | solution.py:285
  17.7 0.0 copy-done.1
  17.7 0.4 %copy-done.2 = bf16[208,256]{1,0:T(8,128)(2,1)} copy-done((bf16[208,256]{1,0:T(8,128)(2,1)}, bf16[208,256]{1,0:T(8,128)(2,1)S(1)}, u32[]{:S(2)}) %copy-start.2) | copy-done | bytes 106520
  18.1 0.0 copy-start.3
  18.1 0.6 %copy-done.3 = bf16[208,256]{1,0:T(8,128)(2,1)} copy-done((bf16[208,256]{1,0:T(8,128)(2,1)}, bf16[208,256]{1,0:T(8,128)(2,1)S(1)}, u32[]{:S(2)}) %copy-start.3) | copy-done | bytes 106520
  18.7 3.0 %finish_and_conv5.1 = (f32[256,128]{1,0:T(8,128)}, f32[256,128]{1,0:T(8,128)}) custom-call(s32[3]{0:T(128)} %pad_add_fusion.at_ref, bf16[208,256]{1,0:T(8,128)(2,1)} %pool_and_pack.1.q0, bf16[208,256]{1,0:T(8,128)(2,1)} %copy-done.3, bf16[208,256]{1,0:T(8,128)(2,1)} %copy-done.2, bf16[208,256]{1,0:T(8,128)(2,1)} %copy-done.1, bf16[3,3,3,256,128]{4,3,2,1,0:T(8,128)(2,1)} %w_ref.5), custom_call_target="tpu_custom_call" | custom-call | flops 301989888 | bytes 1179648 | tf_op jit(solution)/shard_map/finish_and_conv5/pallas_call | solution.py:328
  21.7 0.0 collective-permute-start.4
  21.8 1.5 %collective-permute-done.4 = f32[256,128]{1,0:T(8,128)S(1)} collective-permute-done((f32[256,128]{1,0:T(8,128)}, f32[256,128]{1,0:T(8,128)S(1)}, u32[]{:S(2)}, u32[]{:S(2)}) %collective-permute-start.4) | collective-permute-done | bytes 131104 | tf_op jit(solution)/shard_map/ppermute | solution.py:285
  23.3 1.6 %add_convert_fusion = bf16[256,128]{1,0:T(8,128)(2,1)} fusion(f32[256,128]{1,0:T(8,128)} %get-tuple-element.11, f32[256,128]{1,0:T(8,128)S(1)} %collective-permute-done.4), kind=kLoop, calls=%fused_computation | loop fusion | flops 65536 | bytes 327680 | tf_op jit(solution)/shard_map/convert_element_type | solution.py:342
Async XLA Ops:
  0.0 4.4 %collective-permute-start = (bf16[2,16,16,128]{3,2,1,0:T(8,128)(2,1)}, bf16[2,16,16,128]{3,2,1,0:T(8,128)(2,1)S(1)}, u32[]{:S(2)}, u32[]{:S(2)}) collective-permute-start(bf16[2,16,16,128]{3,2,1,0:T(8,128)(2,1)} %v_ref.1), channel_id=1, source_target_pairs={{0,4},{1,5},{2,6},{3,7},{4,0},{5,1},{6,2},{7,3},{8,12},{9,13},{10,... | collective-permute-start | bytes 393224 | tf_op jit(solution)/shard_map/ppermute | solution.py:285
  4.4 0.7 %copy-start = (bf16[2,16,16,128]{3,2,1,0:T(8,128)(2,1)}, bf16[2,16,16,128]{3,2,1,0:T(8,128)(2,1)S(1)}, u32[]{:S(2)}) copy-start(bf16[2,16,16,128]{3,2,1,0:T(8,128)(2,1)S(1)} %collective-permute-done.r_ref) | copy-start | bytes 393220
  7.9 7.4 %collective-permute-start.3 = (bf16[208,256]{1,0:T(8,128)(2,1)}, bf16[208,256]{1,0:T(8,128)(2,1)S(1)}, u32[]{:S(2)}, u32[]{:S(2)}) collective-permute-start(bf16[208,256]{1,0:T(8,128)(2,1)} %pool_and_pack.1.q0), channel_id=1, source_target_pairs={{0,3},{1,2},{2,1},{3,0},{4,7},{5,6},{6,5},{7,4},{8,11},{9,10},{10,... | collective-permute-start | bytes 319496 | tf_op jit(solution)/shard_map/ppermute | solution.py:285
  11.3 6.1 %collective-permute-start.2 = (bf16[208,256]{1,0:T(8,128)(2,1)}, bf16[208,256]{1,0:T(8,128)(2,1)S(1)}, u32[]{:S(2)}, u32[]{:S(2)}) collective-permute-start(bf16[208,256]{1,0:T(8,128)(2,1)} %pool_and_pack.1.q0), channel_id=1, source_target_pairs={{0,1},{1,0},{2,3},{3,2},{4,5},{5,4},{6,7},{7,6},{8,9},{9,8},{10,11... | collective-permute-start | bytes 319496 | tf_op jit(solution)/shard_map/ppermute | solution.py:285
  11.8 5.9 %collective-permute-start.1 = (bf16[208,256]{1,0:T(8,128)(2,1)}, bf16[208,256]{1,0:T(8,128)(2,1)S(1)}, u32[]{:S(2)}, u32[]{:S(2)}) collective-permute-start(bf16[208,256]{1,0:T(8,128)(2,1)} %pool_and_pack.1.q0), channel_id=1, source_target_pairs={{0,2},{1,3},{2,0},{3,1},{4,6},{5,7},{6,4},{7,5},{8,10},{9,11},{10,... | collective-permute-start | bytes 319496 | tf_op jit(solution)/shard_map/ppermute | solution.py:285
  15.3 2.5 %copy-start.1 = (bf16[208,256]{1,0:T(8,128)(2,1)}, bf16[208,256]{1,0:T(8,128)(2,1)S(1)}, u32[]{:S(2)}) copy-start(bf16[208,256]{1,0:T(8,128)(2,1)S(1)} %collective-permute-done.3.q3) | copy-start | bytes 319492
  17.5 0.6 %copy-start.2 = (bf16[208,256]{1,0:T(8,128)(2,1)}, bf16[208,256]{1,0:T(8,128)(2,1)S(1)}, u32[]{:S(2)}) copy-start(bf16[208,256]{1,0:T(8,128)(2,1)S(1)} %collective-permute-done.2.q2) | copy-start | bytes 319492
  18.1 0.6 %copy-start.3 = (bf16[208,256]{1,0:T(8,128)(2,1)}, bf16[208,256]{1,0:T(8,128)(2,1)S(1)}, u32[]{:S(2)}) copy-start(bf16[208,256]{1,0:T(8,128)(2,1)S(1)} %collective-permute-done.1.q1) | copy-start | bytes 319492
  21.7 1.6 %collective-permute-start.4 = (f32[256,128]{1,0:T(8,128)}, f32[256,128]{1,0:T(8,128)S(1)}, u32[]{:S(2)}, u32[]{:S(2)}) collective-permute-start(f32[256,128]{1,0:T(8,128)} %get-tuple-element.12), channel_id=1, source_target_pairs={{0,4},{1,5},{2,6},{3,7},{4,0},{5,1},{6,2},{7,3},{8,12},{9,13},{10,... | collective-permute-start | bytes 393224 | tf_op jit(solution)/shard_map/ppermute | solution.py:285

commit v2 on v1

--- a/solution.py
+++ b/solution.py
@@ -10,8 +10,9 @@
 BF = jnp.bfloat16
 F32 = jnp.float32
 VMEM = pl.BlockSpec(memory_space=pltpu.VMEM)
-SMEM = pl.BlockSpec(memory_space=pltpu.SMEM)
+HBM = pl.BlockSpec(memory_space=pltpu.HBM)
 GROUP = ("gx", "gy", "gz")
+PARAMS = pltpu.CompilerParams(vmem_limit_bytes=8 * 2**20)
 
 
 def extended(cells, sides, width):
@@ -117,30 +118,44 @@
     return jnp.concatenate([w_ref[dx, dy, 2 * at_z] for dy in range(taps)], axis=0)
 
 
-def own_kernel(at_ref, v_ref, w_ref, h_ref, t_ref, shift_ref, flat_ref, col_ref):
-    at_y, at_z = at_ref[1], at_ref[2]
+def own_kernel(v_hbm, w_hbm, h_ref, t_ref, w_ref, v_ref, shift_ref, flat_ref, col_ref, w_sem, v_sem):
+    load = pltpu.make_async_copy(v_hbm, v_ref, v_sem)
+    load.start()
+    order = (1, 0, 2)
+    loads = {dx: pltpu.make_async_copy(w_hbm.at[dx], w_ref.at[dx], w_sem.at[dx]) for dx in order}
+    for dx in order:
+        loads[dx].start()
+    at_y, at_z = lax.axis_index("gy"), lax.axis_index("gz")
     planes, ny, nz, nc = v_ref.shape
     filters = w_ref.shape[4]
+    load.wait()
     for p in range(planes):
         shifted_copies(v_ref[p], shift_ref, p)
     wins = [windows(shift_ref, p, 1 - at_y, ny) for p in range(planes)]
-    for p in range(planes):
-        lhs = jnp.concatenate(wins, axis=1)
-        rhs = w_ref[1 - p : 3 - p].reshape(2 * 9 * nc, filters)
-        h_ref[p] = jnp.dot(lhs, rhs, preferred_element_type=F32).reshape(h_ref.shape[1:])
     edges = [edge_windows(v_ref[p], flat_ref, col_ref, p, at_y, at_z) for p in range(planes)]
-    lhs = jnp.concatenate(edges, axis=1)
-    for p in range(planes):
-        rhs = jnp.concatenate([edge_weights(w_ref, 1 - p, at_z), edge_weights(w_ref, 2 - p, at_z)], axis=0)
-        t_ref[p] = jnp.dot(lhs, rhs, preferred_element_type=F32)
+    for dx in order:
+        loads[dx].wait()
+        for p in range(planes):
+            source = p + dx - 1
+            if not 0 <= source < planes:
+                continue
+            rhs = w_ref[dx].reshape(9 * nc, filters)
+            sums = jnp.dot(wins[source], rhs, preferred_element_type=F32).reshape(h_ref.shape[1:])
+            past = jnp.dot(edges[source], edge_weights(w_ref, dx, at_z), preferred_element_type=F32)
+            if dx == order[0]:
+                h_ref[p] = sums
+                t_ref[p] = past
+            else:
+                h_ref[p] += sums
+                t_ref[p] += past
 
 
 def put(out_ref, first, rows):
     out_ref[first : first + rows.shape[0]] = rows.astype(out_ref.dtype)
 
 
-def pack_kernel(at_ref, r_ref, w_ref, h_in, t_in, out_ref, h_ref, t_ref, shift_ref, flat_ref, col_ref, pair_ref):
-    at_x, at_y, at_z = at_ref[0], at_ref[1], at_ref[2]
+def pack_kernel(r_ref, w_ref, h_in, t_in, out_ref, h_ref, t_ref, shift_ref, flat_ref, col_ref, pair_ref):
+    at_x, at_y, at_z = (lax.axis_index(axis) for axis in GROUP)
     planes, ny, nz, nc = r_ref.shape
     filters = w_ref.shape[4]
     plane = r_ref[at_x]
@@ -160,6 +175,7 @@
         return h_ref[pl.ds(pl.multiple_of((p * (ny + 1) + e) * nz, 8), nz)]
 
     low = -jnp.inf
+    y_edge = lax.broadcasted_iota(jnp.int32, (ny, filters), 0) == (ny - 1) * (1 - at_y)
     is_edge = lax.broadcasted_iota(jnp.int32, (nz, filters), 0) == (nz - 1) * (1 - at_z)
     for k in range(ny // 2):
         first = jnp.maximum(row(0, at_y + 2 * k), row(1, at_y + 2 * k))
@@ -199,17 +215,15 @@
                     jnp.where(at_z == 0, picks[3], picks[2]),
                 )
             )
-        put(out_ref, base + p * ny, jnp.concatenate(column, axis=1))
+        corner = jnp.where(at_y == 0, t_ref[p, ny : ny + 1], t_ref[p, 0:1])
+        column = jnp.where(y_edge, corner, jnp.concatenate(column, axis=1))
+        put(out_ref, base + p * ny, column)
         base += planes * ny
         put(out_ref, base + p * ny, jnp.where(at_y == 0, t_ref[p, 0:ny], t_ref[p, 1 : ny + 1]))
-    base += planes * ny
-    corner = jnp.where(at_y == 0, t_ref[:, ny : ny + 1], t_ref[:, 0:1])
-    at = lax.broadcasted_iota(jnp.int32, (16, filters), 0)
-    put(out_ref, base, jnp.where(at == 0, corner[0], jnp.where(at == 1, corner[1], 0.0)))
-
-
-def finish_kernel(at_ref, q0, q1, q2, q3, w_ref, own_ref, other_ref, pack_ref, full_ref, pair_ref, shift_ref, *, ny, nz, planes):
-    at_x, at_y, at_z = at_ref[0], at_ref[1], at_ref[2]
+
+
+def finish_kernel(q0, q1, q2, q3, w_ref, own_ref, other_ref, pack_ref, full_ref, pair_ref, shift_ref, *, ny, nz, planes):
+    at_x, at_y, at_z = (lax.axis_index(axis) for axis in GROUP)
     filters = w_ref.shape[3]
     outs = w_ref.shape[4]
     here = 2 * at_y + at_z
@@ -223,7 +237,6 @@
     over_y = row_at + planes * nz
     col_at = over_y + planes * nz
     over_z = col_at + planes * ny
-    over_c = over_z + planes * ny
 
     def take(q, first, count):
         return pack_ref[q, first : first + count].astype(F32)
@@ -242,12 +255,12 @@
         for qz in range(2):
             q, by_y, by_z, by_both = 2 * qy + qz, 2 * (1 - qy) + qz, 2 * qy + 1 - qz, 2 * (1 - qy) + 1 - qz
             y_edge, z_edge = (ny - 1) * (1 - qy), (nz - 1) * (1 - qz)
-            corner = take(by_both, over_c, 16)
             edge_row, edge_col = None, None
             at = lax.broadcasted_iota(jnp.int32, (nz, filters), 0)
             for p in range(planes):
                 across = take(by_z, over_z + p * ny, ny)
-                extra = across[y_edge : y_edge + 1] + corner[p : p + 1]
+                corner = take(by_both, col_at + p * ny, ny)[ny - 1 - y_edge : ny - y_edge]
+                extra = across[y_edge : y_edge + 1] + corner
                 line = take(q, row_at + p * nz, nz) + take(by_y, over_y + p * nz, nz)
                 line = jnp.where(at == z_edge, line + extra, line)
                 edge_row = line if edge_row is None else jnp.maximum(edge_row, line)
@@ -276,10 +289,13 @@
     other_ref[...] = sums[:, outs:]
 
 
+def add_kernel(own_ref, other_ref, out_ref):
+    out_ref[...] = (own_ref[...] + other_ref[...]).astype(out_ref.dtype)
+
+
 def pair_body(volume, conv4_weight, conv5_weight):
     planes, ny, nz, nc = volume.shape
     f4, f5 = conv4_weight.shape[4], conv5_weight.shape[4]
-    at = jnp.stack([lax.axis_index(axis) for axis in GROUP]).astype(jnp.int32)
 
     def swap(x, flips):
         return lax.ppermute(x, GROUP, [(i, i ^ flips) for i in range(8)])
@@ -287,28 +303,33 @@
     cost = functools.partial(pl.CostEstimate, transcendentals=0)
     rows = (ny + 1) * nz
     theirs = swap(volume, 4)
-    hidden, past = pl.pallas_call(
+    hidden, past, kernel4 = pl.pallas_call(
         own_kernel,
         out_shape=(
             jax.ShapeDtypeStruct((planes, ny + 1, nz, f4), F32),
             jax.ShapeDtypeStruct((planes, ny + 8, f4), F32),
+            jax.ShapeDtypeStruct(conv4_weight.shape, BF),
         ),
-        in_specs=[SMEM, VMEM, VMEM],
-        out_specs=(VMEM, VMEM),
+        in_specs=[HBM, HBM],
+        out_specs=(VMEM, VMEM, VMEM),
         scratch_shapes=[
+            pltpu.VMEM(volume.shape, BF),
             pltpu.VMEM((3, planes, ny + 4, nz, nc), BF),
             pltpu.VMEM((planes, ny * nz, nc), F32),
             pltpu.VMEM((planes, ny + 24, nc), F32),
+            pltpu.SemaphoreType.DMA((3,)),
+            pltpu.SemaphoreType.DMA,
         ],
         cost_estimate=cost(flops=2 * planes * rows * 18 * nc * f4, bytes_accessed=54 * nc * f4),
+        compiler_params=PARAMS,
         name="own_planes",
-    )(at, volume, conv4_weight)
+    )(*(pltpu.with_memory_space_constraint(x, pltpu.HBM) for x in (volume, conv4_weight)))
     cells = ny * nz // 4
-    packed = cells + planes * (2 * nz + 2 * ny) + 16
+    packed = cells + planes * (2 * nz + 2 * ny)
     pack = pl.pallas_call(
         pack_kernel,
         out_shape=jax.ShapeDtypeStruct((packed, f4), BF),
-        in_specs=[SMEM, VMEM, VMEM, VMEM, VMEM],
+        in_specs=[VMEM] * 4,
         out_specs=VMEM,
         scratch_shapes=[
             pltpu.VMEM((planes * rows, f4), F32),
@@ -319,8 +340,9 @@
             pltpu.VMEM((f4 // 128, rows, 128), F32),
         ],
         cost_estimate=cost(flops=2 * rows * 9 * nc * f4, bytes_accessed=18 * nc * f4),
+        compiler_params=PARAMS,
         name="pool_and_pack",
-    )(at, theirs, conv4_weight, hidden, past)
+    )(theirs, kernel4, hidden, past)
     by_y = swap(pack, 2)
     by_z = swap(pack, 1)
     by_both = swap(pack, 3)
@@ -328,7 +350,7 @@
     own, other = pl.pallas_call(
         functools.partial(finish_kernel, ny=ny, nz=nz, planes=planes),
         out_shape=(jax.ShapeDtypeStruct((gy * gz, f5), F32), jax.ShapeDtypeStruct((gy * gz, f5), F32)),
-        in_specs=[SMEM] + [VMEM] * 5,
+        in_specs=[VMEM] * 5,
         out_specs=(VMEM, VMEM),
         scratch_shapes=[
             pltpu.VMEM((4, packed, f4), BF),
@@ -337,9 +359,17 @@
             pltpu.VMEM((3, 1, gy + 4, gz, f4), BF),
         ],
         cost_estimate=cost(flops=4 * gy * gz * 9 * f4 * f5, bytes_accessed=36 * f4 * f5),
+        compiler_params=PARAMS,
         name="finish_and_conv5",
-    )(at, pack, by_y, by_z, by_both, conv5_weight)
-    features = (own + swap(other, 4)).astype(BF)
+    )(pack, by_y, by_z, by_both, conv5_weight)
+    features = pl.pallas_call(
+        add_kernel,
+        out_shape=jax.ShapeDtypeStruct((gy * gz, f5), BF),
+        in_specs=[VMEM] * 2,
+        out_specs=VMEM,
+        compiler_params=PARAMS,
+        name="add_planes",
+    )(own, swap(other, 4))
     return features.reshape(1, gy, gz, f5)
 
 

time: 25.1 us -> 16.3 us (0.65)
  Pallas kernels: 9.14 us -> 4.89 us
  other arithmetic: 2.21 us -> 0 us
  local copies, waits for them, and re-layouts: 1.64 us -> 0.01 us
  waiting for transfers between devices: 7.35 us -> 6.52 us
    pallas_call x1, Pallas kernels: 3 us -> 0.6 us  [pair_body(): pl.pallas_call(functools.partial(finish_kernel, ny=ny, nz=nz, planes=plan...]
    pallas_call x1, Pallas kernels: 2.8 us -> 0.6 us  [pair_body(): pl.pallas_call(pack_kernel, out_shape=jax.ShapeDtypeStruct((packed, f4),...]
    unnamed x8 -> x2, local copies, waits for them, and re-layouts: 1.64 us -> 0.01 us
    convert_element_type x1 -> x0, other arithmetic: 1.56 us -> none  [pair_body(): features = (own + swap(other, 4)).astype(BF)]
    ppermute x5, waiting for transfers between devices: 7.35 us -> 6.52 us  [swap(): return lax.ppermute(x, GROUP, [(i, i ^ flips) for i in range(8)])]
    another operation x1 -> x0, other arithmetic: 0.65 us -> none  [pair_body(): at = jnp.stack([lax.axis_index(axis) for axis in GROUP]).astype(jnp.int32)]
    pallas_call x0 -> x1, Pallas kernels: none -> 0.64 us  [pair_body(): pl.pallas_call(add_kernel, out_shape=jax.ShapeDtypeStruct((gy * gz, f5),...]
    pallas_call x1, Pallas kernels: 3.34 us -> 3.04 us  [pair_body(): pl.pallas_call(own_kernel, out_shape=(jax.ShapeDtypeStruct((planes, ny +...]
  transfers between devices with their start and end apart: 5 -> 5, of which waited for: 4 -> 4; matrix products, arithmetic and copies ran while one was open for 3% -> 0% of each run, Pallas kernels for 13% -> 19%
where the time goes in v2:
time: 16.3 us; the launch traced here: 16.1 us
  waiting for transfers between devices  6.52 us (40%)
  Pallas kernels  4.89 us (30%)
  starting transfers between devices  4.67 us (29%)
    ppermute x5, waiting for transfers between devices, swap(): return lax.ppermute(x, GROUP, [(i, i ^ flips) for i in range(8)])  6.52 us
    ppermute x5, starting transfers between devices, swap(): return lax.ppermute(x, GROUP, [(i, i ^ flips) for i in range(8)])  4.67 us
    pallas_call x1, Pallas kernels, pair_body(): pl.pallas_call(own_kernel, out_shape=(jax.ShapeDtypeStruct((planes, ny +...  3.04 us
    pallas_call x1, Pallas kernels, pair_body(): pl.pallas_call(add_kernel, out_shape=jax.ShapeDtypeStruct((gy * gz, f5),...  0.64 us
    pallas_call x1, Pallas kernels, pair_body(): pl.pallas_call(pack_kernel, out_shape=jax.ShapeDtypeStruct((packed, f4),...  0.6 us
    pallas_call x1, Pallas kernels, pair_body(): pl.pallas_call(functools.partial(finish_kernel, ny=ny, nz=nz, planes=plan...  0.6 us
  transfers between devices with their start and end apart: 5, of which 4 were waited for; matrix products, arithmetic and copies ran while one was open for 0% of the time, Pallas kernels for 19%

profile of v2, /device:TPU:0, one launch (start us, length us, event | category | flops | bytes accessed | tf_op | source)
XLA Modules:
  0.0 16.1 jit_solution(14555249842980746909)
XLA Ops:
  0.0 0.5 %collective-permute-start = (bf16[2,16,16,128]{3,2,1,0:T(8,128)(2,1)}, bf16[2,16,16,128]{3,2,1,0:T(8,128)(2,1)S(1)}, u32[]{:S(2)}, u32[]{:S(2)}) collective-permute-start(bf16[2,16,16,128]{3,2,1,0:T(8,128)(2,1)} %v_hbm.1), channel_id=1, source_target_pairs={{0,4},{1,5},{2,6},{3,7},{4,0},{5,1},{6,2},{7,3},{8,12},{9,13},{10,... | collective-permute-start | bytes 393224 | tf_op jit(solution)/shard_map/ppermute | solution.py:301
  0.5 3.0 %own_planes.1 = (f32[2,17,16,256]{3,2,1,0:T(8,128)S(1)}, f32[2,24,256]{2,1,0:T(8,128)S(1)}, bf16[3,3,3,128,256]{4,3,2,1,0:T(8,128)(2,1)S(1)}) custom-call(bf16[2,16,16,128]{3,2,1,0:T(8,128)(2,1)} %v_hbm.1, bf16[3,3,3,128,256]{4,3,2,1,0:T(8,128)(2,1)} %w_hbm.1), custom_call_target="tpu_custom_call" | custom-call | flops 641728512 | bytes 1769472 | tf_op jit(solution)/shard_map/own_planes/pallas_call | solution.py:306
  3.5 0.0 copy-start
  3.5 0.0 collective-permute-done.r_ref
  3.5 0.6 %pool_and_pack.1.q0 = bf16[192,256]{1,0:T(8,128)(2,1)S(1)} custom-call(bf16[2,16,16,128]{3,2,1,0:T(8,128)(2,1)S(1)} %collective-permute-done.r_ref, bf16[3,3,3,128,256]{4,3,2,1,0:T(8,128)(2,1)S(1)} %get-tuple-element.10.w_ref, f32[2,17,16,256]{3,2,1,0:T(8,128)S(1)} %get-tuple-element.11.h_in, f32[2,24,256]{2,1,0:T(8,128)S(1)} %get-tuple-element.12.t_in), custom_call_target="tpu_custom_call" | custom-call | flops 160432128 | bytes 589824 | tf_op jit(solution)/shard_map/pool_and_pack/pallas_call | solution.py:329
  4.1 3.5 %collective-permute-start.3 = (bf16[192,256]{1,0:T(8,128)(2,1)S(1)}, bf16[192,256]{1,0:T(8,128)(2,1)S(1)}, u32[]{:S(2)}, u32[]{:S(2)}) collective-permute-start(bf16[192,256]{1,0:T(8,128)(2,1)S(1)} %pool_and_pack.1.q0), channel_id=1, source_target_pairs={{0,3},{1,2},{2,1},{3,0},{4,7},{5,6},{6,5},{7,4},{8,11},{9,10},{10,... | collective-permute-start | bytes 294920 | tf_op jit(solution)/shard_map/ppermute | solution.py:301
  7.6 0.5 %collective-permute-start.2 = (bf16[192,256]{1,0:T(8,128)(2,1)S(1)}, bf16[192,256]{1,0:T(8,128)(2,1)S(1)}, u32[]{:S(2)}, u32[]{:S(2)}) collective-permute-start(bf16[192,256]{1,0:T(8,128)(2,1)S(1)} %pool_and_pack.1.q0), channel_id=1, source_target_pairs={{0,1},{1,0},{2,3},{3,2},{4,5},{5,4},{6,7},{7,6},{8,9},{9,8},{10,11... | collective-permute-start | bytes 294920 | tf_op jit(solution)/shard_map/ppermute | solution.py:301
  8.1 0.1 collective-permute-start.1
  8.3 2.9 %collective-permute-done.3.q3 = bf16[192,256]{1,0:T(8,128)(2,1)S(1)} collective-permute-done((bf16[192,256]{1,0:T(8,128)(2,1)S(1)}, bf16[192,256]{1,0:T(8,128)(2,1)S(1)}, u32[]{:S(2)}, u32[]{:S(2)}) %collective-permute-start.3) | collective-permute-done | bytes 98336 | tf_op jit(solution)/shard_map/ppermute | solution.py:301
  11.2 2.0 %collective-permute-done.2.q2 = bf16[192,256]{1,0:T(8,128)(2,1)S(1)} collective-permute-done((bf16[192,256]{1,0:T(8,128)(2,1)S(1)}, bf16[192,256]{1,0:T(8,128)(2,1)S(1)}, u32[]{:S(2)}, u32[]{:S(2)}) %collective-permute-start.2) | collective-permute-done | bytes 98336 | tf_op jit(solution)/shard_map/ppermute | solution.py:301
  13.2 0.3 %collective-permute-done.1.q1 = bf16[192,256]{1,0:T(8,128)(2,1)S(1)} collective-permute-done((bf16[192,256]{1,0:T(8,128)(2,1)S(1)}, bf16[192,256]{1,0:T(8,128)(2,1)S(1)}, u32[]{:S(2)}, u32[]{:S(2)}) %collective-permute-start.1) | collective-permute-done | bytes 98336 | tf_op jit(solution)/shard_map/ppermute | solution.py:301
  13.5 0.0 copy-done
  13.5 0.6 %finish_and_conv5.1 = (f32[256,128]{1,0:T(8,128)S(1)}, f32[256,128]{1,0:T(8,128)S(1)}) custom-call(bf16[192,256]{1,0:T(8,128)(2,1)S(1)} %pool_and_pack.1.q0, bf16[192,256]{1,0:T(8,128)(2,1)S(1)} %collective-permute-done.1.q1, bf16[192,256]{1,0:T(8,128)(2,1)S(1)} %collective-permute-done.2.q2, bf16[192,256]{1,0:T(8,128)(2,1)S(1)} %collective-permute-done.3.q3, ...), custom_call_target="tpu_custom_call" | custom-call | flops 301989888 | bytes 1179648 | tf_op jit(solution)/shard_map/finish_and_conv5/pallas_call | solution.py:350
  14.1 0.1 collective-permute-start.4
  14.2 1.3 %collective-permute-done.4.other_ref = f32[256,128]{1,0:T(8,128)S(1)} collective-permute-done((f32[256,128]{1,0:T(8,128)S(1)}, f32[256,128]{1,0:T(8,128)S(1)}, u32[]{:S(2)}, u32[]{:S(2)}) %collective-permute-start.4) | collective-permute-done | bytes 131104 | tf_op jit(solution)/shard_map/ppermute | solution.py:301
  15.5 0.6 %add_planes.1 = bf16[256,128]{1,0:T(8,128)(2,1)} custom-call(f32[256,128]{1,0:T(8,128)S(1)} %get-tuple-element.13.own_ref, f32[256,128]{1,0:T(8,128)S(1)} %collective-permute-done.4.other_ref), custom_call_target="tpu_custom_call" | custom-call | tf_op jit(solution)/shard_map/add_planes/pallas_call | solution.py:365
Async XLA Ops:
  0.0 3.5 %collective-permute-start = (bf16[2,16,16,128]{3,2,1,0:T(8,128)(2,1)}, bf16[2,16,16,128]{3,2,1,0:T(8,128)(2,1)S(1)}, u32[]{:S(2)}, u32[]{:S(2)}) collective-permute-start(bf16[2,16,16,128]{3,2,1,0:T(8,128)(2,1)} %v_hbm.1), channel_id=1, source_target_pairs={{0,4},{1,5},{2,6},{3,7},{4,0},{5,1},{6,2},{7,3},{8,12},{9,13},{10,... | collective-permute-start | bytes 393224 | tf_op jit(solution)/shard_map/ppermute | solution.py:301
  3.5 10.0 %copy-start = (bf16[3,3,3,256,128]{4,3,2,1,0:T(8,128)(2,1)S(1)}, bf16[3,3,3,256,128]{4,3,2,1,0:T(8,128)(2,1)}, u32[]{:S(2)}) copy-start(bf16[3,3,3,256,128]{4,3,2,1,0:T(8,128)(2,1)} %w_ref.1) | copy-start | bytes 5308420
  4.1 7.0 %collective-permute-start.3 = (bf16[192,256]{1,0:T(8,128)(2,1)S(1)}, bf16[192,256]{1,0:T(8,128)(2,1)S(1)}, u32[]{:S(2)}, u32[]{:S(2)}) collective-permute-start(bf16[192,256]{1,0:T(8,128)(2,1)S(1)} %pool_and_pack.1.q0), channel_id=1, source_target_pairs={{0,3},{1,2},{2,1},{3,0},{4,7},{5,6},{6,5},{7,4},{8,11},{9,10},{10,... | collective-permute-start | bytes 294920 | tf_op jit(solution)/shard_map/ppermute | solution.py:301
  7.6 5.6 %collective-permute-start.2 = (bf16[192,256]{1,0:T(8,128)(2,1)S(1)}, bf16[192,256]{1,0:T(8,128)(2,1)S(1)}, u32[]{:S(2)}, u32[]{:S(2)}) collective-permute-start(bf16[192,256]{1,0:T(8,128)(2,1)S(1)} %pool_and_pack.1.q0), channel_id=1, source_target_pairs={{0,1},{1,0},{2,3},{3,2},{4,5},{5,4},{6,7},{7,6},{8,9},{9,8},{10,11... | collective-permute-start | bytes 294920 | tf_op jit(solution)/shard_map/ppermute | solution.py:301
  8.1 5.3 %collective-permute-start.1 = (bf16[192,256]{1,0:T(8,128)(2,1)S(1)}, bf16[192,256]{1,0:T(8,128)(2,1)S(1)}, u32[]{:S(2)}, u32[]{:S(2)}) collective-permute-start(bf16[192,256]{1,0:T(8,128)(2,1)S(1)} %pool_and_pack.1.q0), channel_id=1, source_target_pairs={{0,2},{1,3},{2,0},{3,1},{4,6},{5,7},{6,4},{7,5},{8,10},{9,11},{10,... | collective-permute-start | bytes 294920 | tf_op jit(solution)/shard_map/ppermute | solution.py:301
  14.1 1.4 %collective-permute-start.4 = (f32[256,128]{1,0:T(8,128)S(1)}, f32[256,128]{1,0:T(8,128)S(1)}, u32[]{:S(2)}, u32[]{:S(2)}) collective-permute-start(f32[256,128]{1,0:T(8,128)S(1)} %get-tuple-element.14), channel_id=1, source_target_pairs={{0,4},{1,5},{2,6},{3,7},{4,0},{5,1},{6,2},{7,3},{8,12},{9,13},{10,... | collective-permute-start | bytes 393224 | tf_op jit(solution)/shard_map/ppermute | solution.py:301

commit v3 on v2

--- a/solution.py
+++ b/solution.py
@@ -118,58 +118,44 @@
     return jnp.concatenate([w_ref[dx, dy, 2 * at_z] for dy in range(taps)], axis=0)
 
 
-def own_kernel(v_hbm, w_hbm, h_ref, t_ref, w_ref, v_ref, shift_ref, flat_ref, col_ref, w_sem, v_sem):
-    load = pltpu.make_async_copy(v_hbm, v_ref, v_sem)
-    load.start()
-    order = (1, 0, 2)
-    loads = {dx: pltpu.make_async_copy(w_hbm.at[dx], w_ref.at[dx], w_sem.at[dx]) for dx in order}
-    for dx in order:
-        loads[dx].start()
+def prepare_kernel(v_hbm, w_hbm, shift_ref, edge_ref, w_ref, v_ref, flat_ref, col_ref, v_sem, w_sem):
+    load_v = pltpu.make_async_copy(v_hbm, v_ref, v_sem)
+    load_w = pltpu.make_async_copy(w_hbm, w_ref, w_sem)
+    load_v.start()
+    load_w.start()
     at_y, at_z = lax.axis_index("gy"), lax.axis_index("gz")
-    planes, ny, nz, nc = v_ref.shape
-    filters = w_ref.shape[4]
-    load.wait()
-    for p in range(planes):
+    load_v.wait()
+    for p in range(v_ref.shape[0]):
         shifted_copies(v_ref[p], shift_ref, p)
-    wins = [windows(shift_ref, p, 1 - at_y, ny) for p in range(planes)]
-    edges = [edge_windows(v_ref[p], flat_ref, col_ref, p, at_y, at_z) for p in range(planes)]
-    for dx in order:
-        loads[dx].wait()
-        for p in range(planes):
-            source = p + dx - 1
-            if not 0 <= source < planes:
-                continue
-            rhs = w_ref[dx].reshape(9 * nc, filters)
-            sums = jnp.dot(wins[source], rhs, preferred_element_type=F32).reshape(h_ref.shape[1:])
-            past = jnp.dot(edges[source], edge_weights(w_ref, dx, at_z), preferred_element_type=F32)
-            if dx == order[0]:
-                h_ref[p] = sums
-                t_ref[p] = past
-            else:
-                h_ref[p] += sums
-                t_ref[p] += past
+        edge_ref[p] = edge_windows(v_ref[p], flat_ref, col_ref, p, at_y, at_z)
+    load_w.wait()
 
 
 def put(out_ref, first, rows):
     out_ref[first : first + rows.shape[0]] = rows.astype(out_ref.dtype)
 
 
-def pack_kernel(r_ref, w_ref, h_in, t_in, out_ref, h_ref, t_ref, shift_ref, flat_ref, col_ref, pair_ref):
+def pack_kernel(r_ref, w_ref, own_ref, edge_ref, out_ref, h_ref, t_ref, shift_ref, flat_ref, col_ref, pair_ref):
     at_x, at_y, at_z = (lax.axis_index(axis) for axis in GROUP)
     planes, ny, nz, nc = r_ref.shape
     filters = w_ref.shape[4]
+    rows = (ny + 1) * nz
     plane = r_ref[at_x]
-    dx, mine = 2 * (1 - at_x), 1 - at_x
+    mine = 1 - at_x
     shifted_copies(plane, shift_ref, 0)
+    edge = edge_windows(plane, flat_ref, col_ref, 0, at_y, at_z)
+    for p in range(planes):
+        lhs = jnp.concatenate([windows(own_ref, source, 1 - at_y, ny) for source in range(planes)], axis=1)
+        rhs = w_ref[1 - p : 3 - p].reshape(2 * 9 * nc, filters)
+        h_ref[p * rows : (p + 1) * rows] = jnp.dot(lhs, rhs, preferred_element_type=F32)
+        lhs = jnp.concatenate([edge_ref[source] for source in range(planes)], axis=1)
+        rhs = jnp.concatenate([edge_weights(w_ref, 1 - p, at_z), edge_weights(w_ref, 2 - p, at_z)], axis=0)
+        t_ref[p] = jnp.dot(lhs, rhs, preferred_element_type=F32)
     lhs = windows(shift_ref, 0, 1 - at_y, ny)
-    rhs = w_ref[dx].reshape(9 * nc, filters)
-    for p in range(planes):
-        h_ref[p * (ny + 1) * nz : (p + 1) * (ny + 1) * nz] = h_in[p].reshape((ny + 1) * nz, filters)
-    begin = pl.multiple_of(mine * (ny + 1) * nz, 8)
-    h_ref[pl.ds(begin, (ny + 1) * nz)] += jnp.dot(lhs, rhs, preferred_element_type=F32)
-    edge = edge_windows(plane, flat_ref, col_ref, 0, at_y, at_z)
-    t_ref[...] = t_in[...]
-    t_ref[mine] += jnp.dot(edge, edge_weights(w_ref, dx, at_z), preferred_element_type=F32)
+    rhs = w_ref[2 * mine].reshape(9 * nc, filters)
+    begin = pl.multiple_of(mine * rows, 8)
+    h_ref[pl.ds(begin, rows)] += jnp.dot(lhs, rhs, preferred_element_type=F32)
+    t_ref[mine] += jnp.dot(edge, edge_weights(w_ref, 2 * mine, at_z), preferred_element_type=F32)
 
     def row(p, e):
         return h_ref[pl.ds(pl.multiple_of((p * (ny + 1) + e) * nz, 8), nz)]
@@ -289,6 +275,12 @@
     other_ref[...] = sums[:, outs:]
 
 
+def load_kernel(from_ref, after_ref, to_ref, sem):
+    load = pltpu.make_async_copy(from_ref, to_ref, sem)
+    load.start()
+    load.wait()
+
+
 def add_kernel(own_ref, other_ref, out_ref):
     out_ref[...] = (own_ref[...] + other_ref[...]).astype(out_ref.dtype)
 
@@ -303,26 +295,25 @@
     cost = functools.partial(pl.CostEstimate, transcendentals=0)
     rows = (ny + 1) * nz
     theirs = swap(volume, 4)
-    hidden, past, kernel4 = pl.pallas_call(
-        own_kernel,
+    moved, edges, kernel4 = pl.pallas_call(
+        prepare_kernel,
         out_shape=(
-            jax.ShapeDtypeStruct((planes, ny + 1, nz, f4), F32),
-            jax.ShapeDtypeStruct((planes, ny + 8, f4), F32),
+            jax.ShapeDtypeStruct((3, planes, ny + 4, nz, nc), BF),
+            jax.ShapeDtypeStruct((planes, ny + 8, 3 * nc), BF),
             jax.ShapeDtypeStruct(conv4_weight.shape, BF),
         ),
         in_specs=[HBM, HBM],
         out_specs=(VMEM, VMEM, VMEM),
         scratch_shapes=[
             pltpu.VMEM(volume.shape, BF),
-            pltpu.VMEM((3, planes, ny + 4, nz, nc), BF),
             pltpu.VMEM((planes, ny * nz, nc), F32),
             pltpu.VMEM((planes, ny + 24, nc), F32),
-            pltpu.SemaphoreType.DMA((3,)),
+            pltpu.SemaphoreType.DMA,
             pltpu.SemaphoreType.DMA,
         ],
-        cost_estimate=cost(flops=2 * planes * rows * 18 * nc * f4, bytes_accessed=54 * nc * f4),
-        compiler_params=PARAMS,
-        name="own_planes",
+        cost_estimate=cost(flops=20 * planes * ny * nz * nc, bytes_accessed=12 * planes * ny * nz * nc),
+        compiler_params=PARAMS,
+        name="prepare",
     )(*(pltpu.with_memory_space_constraint(x, pltpu.HBM) for x in (volume, conv4_weight)))
     cells = ny * nz // 4
     packed = cells + planes * (2 * nz + 2 * ny)
@@ -339,10 +330,20 @@
             pltpu.VMEM((1, ny + 24, nc), F32),
             pltpu.VMEM((f4 // 128, rows, 128), F32),
         ],
-        cost_estimate=cost(flops=2 * rows * 9 * nc * f4, bytes_accessed=18 * nc * f4),
-        compiler_params=PARAMS,
-        name="pool_and_pack",
-    )(theirs, kernel4, hidden, past)
+        cost_estimate=cost(flops=5 * 2 * rows * 9 * nc * f4, bytes_accessed=54 * nc * f4),
+        compiler_params=PARAMS,
+        name="conv4_pool_pack",
+    )(theirs, kernel4, moved, edges)
+    kernel5 = pl.pallas_call(
+        load_kernel,
+        out_shape=jax.ShapeDtypeStruct(conv5_weight.shape, BF),
+        in_specs=[HBM, VMEM],
+        out_specs=VMEM,
+        scratch_shapes=[pltpu.SemaphoreType.DMA],
+        cost_estimate=cost(flops=0, bytes_accessed=108 * f4 * f5),
+        compiler_params=PARAMS,
+        name="load_conv5_weight",
+    )(pltpu.with_memory_space_constraint(conv5_weight, pltpu.HBM), pack)
     by_y = swap(pack, 2)
     by_z = swap(pack, 1)
     by_both = swap(pack, 3)
@@ -361,7 +362,7 @@
         cost_estimate=cost(flops=4 * gy * gz * 9 * f4 * f5, bytes_accessed=36 * f4 * f5),
         compiler_params=PARAMS,
         name="finish_and_conv5",
-    )(pack, by_y, by_z, by_both, conv5_weight)
+    )(pack, by_y, by_z, by_both, kernel5)
     features = pl.pallas_call(
         add_kernel,
         out_shape=jax.ShapeDtypeStruct((gy * gz, f5), BF),

time: 16.3 us -> 15.6 us (0.957)
  waiting for transfers between devices: 6.52 us -> 5.03 us
  Pallas kernels: 4.89 us -> 5.68 us
    ppermute x5, waiting for transfers between devices: 6.52 us -> 5.03 us  [swap(): return lax.ppermute(x, GROUP, [(i, i ^ flips) for i in range(8)])]
    pallas_call x1, Pallas kernels: 0.6 us -> 1.38 us  [pair_body(): pl.pallas_call(pack_kernel, out_shape=jax.ShapeDtypeStruct((packed, f4),...]
    pallas_call x1 -> x2, Pallas kernels: 3.04 us -> 3.05 us  [the longest x1 1.57 us: pair_body(): pl.pallas_call(prepare_kernel, out_shape=(jax.ShapeDtypeStruct((3, planes...]
  transfers between devices with their start and end apart: 5 -> 5, of which waited for: 4 -> 4; matrix products, arithmetic and copies ran while one was open for 0% -> 0% of each run, Pallas kernels for 19% -> 20%
where the time goes in v3:
time: 15.6 us; the launch traced here: 15.4 us
  Pallas kernels  5.68 us (36%)
  waiting for transfers between devices  5.03 us (32%)
  starting transfers between devices  4.67 us (30%)
    ppermute x5, waiting for transfers between devices, swap(): return lax.ppermute(x, GROUP, [(i, i ^ flips) for i in range(8)])  5.03 us
    ppermute x5, starting transfers between devices, swap(): return lax.ppermute(x, GROUP, [(i, i ^ flips) for i in range(8)])  4.67 us
    pallas_call x1, Pallas kernels, pair_body(): pl.pallas_call(prepare_kernel, out_shape=(jax.ShapeDtypeStruct((3, planes...  1.57 us
    pallas_call x1, Pallas kernels, pair_body(): pl.pallas_call(load_kernel, out_shape=jax.ShapeDtypeStruct(conv5_weight.s...  1.48 us
    pallas_call x1, Pallas kernels, pair_body(): pl.pallas_call(pack_kernel, out_shape=jax.ShapeDtypeStruct((packed, f4),...  1.38 us
    pallas_call x1, Pallas kernels, pair_body(): pl.pallas_call(add_kernel, out_shape=jax.ShapeDtypeStruct((gy * gz, f5),...  0.64 us
    pallas_call x1, Pallas kernels, pair_body(): pl.pallas_call(functools.partial(finish_kernel, ny=ny, nz=nz, planes=plan...  0.6 us
  transfers between devices with their start and end apart: 5, of which 4 were waited for; matrix products, arithmetic and copies ran while one was open for 0% of the time, Pallas kernels for 20%

profile of v3, /device:TPU:0, one launch (start us, length us, event | category | flops | bytes accessed | tf_op | source)
XLA Modules:
  0.0 15.4 jit_solution(13224042048506971570)
XLA Ops:
  0.0 0.5 %collective-permute-start = (bf16[2,16,16,128]{3,2,1,0:T(8,128)(2,1)}, bf16[2,16,16,128]{3,2,1,0:T(8,128)(2,1)S(1)}, u32[]{:S(2)}, u32[]{:S(2)}) collective-permute-start(bf16[2,16,16,128]{3,2,1,0:T(8,128)(2,1)} %v_hbm.1), channel_id=1, source_target_pairs={{0,4},{1,5},{2,6},{3,7},{4,0},{5,1},{6,2},{7,3},{8,12},{9,13},{10,... | collective-permute-start | bytes 393224 | tf_op jit(solution)/shard_map/ppermute | solution.py:293
  0.5 1.6 %prepare.1 = (bf16[3,2,20,16,128]{4,3,2,1,0:T(8,128)(2,1)S(1)}, bf16[2,24,384]{2,1,0:T(8,128)(2,1)S(1)}, bf16[3,3,3,128,256]{4,3,2,1,0:T(8,128)(2,1)S(1)}) custom-call(bf16[2,16,16,128]{3,2,1,0:T(8,128)(2,1)} %v_hbm.1, bf16[3,3,3,128,256]{4,3,2,1,0:T(8,128)(2,1)} %w_hbm.1), custom_call_target="tpu_custom_call" | custom-call | flops 1310720 | bytes 786432 | tf_op jit(solution)/shard_map/prepare/pallas_call | solution.py:298
  2.0 0.0 collective-permute-done.r_ref
  2.0 1.4 %conv4_pool_pack.1.after_ref.q0 = bf16[192,256]{1,0:T(8,128)(2,1)S(1)} custom-call(bf16[2,16,16,128]{3,2,1,0:T(8,128)(2,1)S(1)} %collective-permute-done.r_ref, bf16[3,3,3,128,256]{4,3,2,1,0:T(8,128)(2,1)S(1)} %get-tuple-element.10.w_ref, bf16[3,2,20,16,128]{4,3,2,1,0:T(8,128)(2,1)S(1)} %get-tuple-element.11.own_ref, ...), custom_call_target="tpu_custom_call" | custom-call | flops 802160640 | bytes 1769472 | tf_op jit(solution)/shard_map/conv4_pool_pack/pallas_call | solution.py:320
  3.4 3.5 %collective-permute-start.3 = (bf16[192,256]{1,0:T(8,128)(2,1)S(1)}, bf16[192,256]{1,0:T(8,128)(2,1)S(1)}, u32[]{:S(2)}, u32[]{:S(2)}) collective-permute-start(bf16[192,256]{1,0:T(8,128)(2,1)S(1)} %conv4_pool_pack.1.after_ref.q0), channel_id=1, source_target_pairs={{0,3},{1,2},{2,1},{3,0},{4,7},{5,6},{6,5},{7,4},{8,11},{9,10},{10,... | collective-permute-start | bytes 294920 | tf_op jit(solution)/shard_map/ppermute | solution.py:293
  6.9 0.5 %collective-permute-start.2 = (bf16[192,256]{1,0:T(8,128)(2,1)S(1)}, bf16[192,256]{1,0:T(8,128)(2,1)S(1)}, u32[]{:S(2)}, u32[]{:S(2)}) collective-permute-start(bf16[192,256]{1,0:T(8,128)(2,1)S(1)} %conv4_pool_pack.1.after_ref.q0), channel_id=1, source_target_pairs={{0,1},{1,0},{2,3},{3,2},{4,5},{5,4},{6,7},{7,6},{8,9},{9,8},{10,11... | collective-permute-start | bytes 294920 | tf_op jit(solution)/shard_map/ppermute | solution.py:293
  7.4 0.1 collective-permute-start.1
  7.6 1.5 %load_conv5_weight.1.w_ref = bf16[3,3,3,256,128]{4,3,2,1,0:T(8,128)(2,1)S(1)} custom-call(bf16[3,3,3,256,128]{4,3,2,1,0:T(8,128)(2,1)} %from_ref.1, bf16[192,256]{1,0:T(8,128)(2,1)S(1)} %conv4_pool_pack.1.after_ref.q0), custom_call_target="tpu_custom_call" | custom-call | bytes 3538944 | tf_op jit(solution)/shard_map/load_conv5_weight/pallas_call | solution.py:337
  9.1 1.4 %collective-permute-done.3.q3 = bf16[192,256]{1,0:T(8,128)(2,1)S(1)} collective-permute-done((bf16[192,256]{1,0:T(8,128)(2,1)S(1)}, bf16[192,256]{1,0:T(8,128)(2,1)S(1)}, u32[]{:S(2)}, u32[]{:S(2)}) %collective-permute-start.3) | collective-permute-done | bytes 98336 | tf_op jit(solution)/shard_map/ppermute | solution.py:293
  10.5 2.0 %collective-permute-done.2.q2 = bf16[192,256]{1,0:T(8,128)(2,1)S(1)} collective-permute-done((bf16[192,256]{1,0:T(8,128)(2,1)S(1)}, bf16[192,256]{1,0:T(8,128)(2,1)S(1)}, u32[]{:S(2)}, u32[]{:S(2)}) %collective-permute-start.2) | collective-permute-done | bytes 98336 | tf_op jit(solution)/shard_map/ppermute | solution.py:293
  12.5 0.3 %collective-permute-done.1.q1 = bf16[192,256]{1,0:T(8,128)(2,1)S(1)} collective-permute-done((bf16[192,256]{1,0:T(8,128)(2,1)S(1)}, bf16[192,256]{1,0:T(8,128)(2,1)S(1)}, u32[]{:S(2)}, u32[]{:S(2)}) %collective-permute-start.1) | collective-permute-done | bytes 98336 | tf_op jit(solution)/shard_map/ppermute | solution.py:293
  12.8 0.6 %finish_and_conv5.1 = (f32[256,128]{1,0:T(8,128)S(1)}, f32[256,128]{1,0:T(8,128)S(1)}) custom-call(bf16[192,256]{1,0:T(8,128)(2,1)S(1)} %conv4_pool_pack.1.after_ref.q0, bf16[192,256]{1,0:T(8,128)(2,1)S(1)} %collective-permute-done.1.q1, bf16[192,256]{1,0:T(8,128)(2,1)S(1)} %collective-permute-done.2.q2, bf16[192,256]{1,0:T(8,128)(2,1)S(1)} %collective-permute-done.3.q3, ...), custom_call_target="tpu_custom_call" | custom-call | flops 301989888 | bytes 1179648 | tf_op jit(solution)/shard_map/finish_and_conv5/pallas_call | solution.py:351
  13.4 0.1 collective-permute-start.4
  13.5 1.3 %collective-permute-done.4.other_ref = f32[256,128]{1,0:T(8,128)S(1)} collective-permute-done((f32[256,128]{1,0:T(8,128)S(1)}, f32[256,128]{1,0:T(8,128)S(1)}, u32[]{:S(2)}, u32[]{:S(2)}) %collective-permute-start.4) | collective-permute-done | bytes 131104 | tf_op jit(solution)/shard_map/ppermute | solution.py:293
  14.8 0.6 %add_planes.1 = bf16[256,128]{1,0:T(8,128)(2,1)} custom-call(f32[256,128]{1,0:T(8,128)S(1)} %get-tuple-element.13.own_ref, f32[256,128]{1,0:T(8,128)S(1)} %collective-permute-done.4.other_ref), custom_call_target="tpu_custom_call" | custom-call | tf_op jit(solution)/shard_map/add_planes/pallas_call | solution.py:366
Async XLA Ops:
  0.0 2.0 %collective-permute-start = (bf16[2,16,16,128]{3,2,1,0:T(8,128)(2,1)}, bf16[2,16,16,128]{3,2,1,0:T(8,128)(2,1)S(1)}, u32[]{:S(2)}, u32[]{:S(2)}) collective-permute-start(bf16[2,16,16,128]{3,2,1,0:T(8,128)(2,1)} %v_hbm.1), channel_id=1, source_target_pairs={{0,4},{1,5},{2,6},{3,7},{4,0},{5,1},{6,2},{7,3},{8,12},{9,13},{10,... | collective-permute-start | bytes 393224 | tf_op jit(solution)/shard_map/ppermute | solution.py:293
  3.4 7.0 %collective-permute-start.3 = (bf16[192,256]{1,0:T(8,128)(2,1)S(1)}, bf16[192,256]{1,0:T(8,128)(2,1)S(1)}, u32[]{:S(2)}, u32[]{:S(2)}) collective-permute-start(bf16[192,256]{1,0:T(8,128)(2,1)S(1)} %conv4_pool_pack.1.after_ref.q0), channel_id=1, source_target_pairs={{0,3},{1,2},{2,1},{3,0},{4,7},{5,6},{6,5},{7,4},{8,11},{9,10},{10,... | collective-permute-start | bytes 294920 | tf_op jit(solution)/shard_map/ppermute | solution.py:293
  6.9 5.6 %collective-permute-start.2 = (bf16[192,256]{1,0:T(8,128)(2,1)S(1)}, bf16[192,256]{1,0:T(8,128)(2,1)S(1)}, u32[]{:S(2)}, u32[]{:S(2)}) collective-permute-start(bf16[192,256]{1,0:T(8,128)(2,1)S(1)} %conv4_pool_pack.1.after_ref.q0), channel_id=1, source_target_pairs={{0,1},{1,0},{2,3},{3,2},{4,5},{5,4},{6,7},{7,6},{8,9},{9,8},{10,11... | collective-permute-start | bytes 294920 | tf_op jit(solution)/shard_map/ppermute | solution.py:293
  7.4 5.3 %collective-permute-start.1 = (bf16[192,256]{1,0:T(8,128)(2,1)S(1)}, bf16[192,256]{1,0:T(8,128)(2,1)S(1)}, u32[]{:S(2)}, u32[]{:S(2)}) collective-permute-start(bf16[192,256]{1,0:T(8,128)(2,1)S(1)} %conv4_pool_pack.1.after_ref.q0), channel_id=1, source_target_pairs={{0,2},{1,3},{2,0},{3,1},{4,6},{5,7},{6,4},{7,5},{8,10},{9,11},{10,... | collective-permute-start | bytes 294920 | tf_op jit(solution)/shard_map/ppermute | solution.py:293
  13.4 1.4 %collective-permute-start.4 = (f32[256,128]{1,0:T(8,128)S(1)}, f32[256,128]{1,0:T(8,128)S(1)}, u32[]{:S(2)}, u32[]{:S(2)}) collective-permute-start(f32[256,128]{1,0:T(8,128)S(1)} %get-tuple-element.14), channel_id=1, source_target_pairs={{0,4},{1,5},{2,6},{3,7},{4,0},{5,1},{6,2},{7,3},{8,12},{9,13},{10,... | collective-permute-start | bytes 393224 | tf_op jit(solution)/shard_map/ppermute | solution.py:293

commit v4 on v3

--- a/solution.py
+++ b/solution.py
@@ -272,13 +272,7 @@
     )
     sums = jnp.dot(lhs, rhs, preferred_element_type=F32)
     own_ref[...] = sums[:, :outs]
-    other_ref[...] = sums[:, outs:]
-
-
-def load_kernel(from_ref, after_ref, to_ref, sem):
-    load = pltpu.make_async_copy(from_ref, to_ref, sem)
-    load.start()
-    load.wait()
+    other_ref[...] = sums[:, outs:].astype(other_ref.dtype)
 
 
 def add_kernel(own_ref, other_ref, out_ref):
@@ -334,23 +328,13 @@
         compiler_params=PARAMS,
         name="conv4_pool_pack",
     )(theirs, kernel4, moved, edges)
-    kernel5 = pl.pallas_call(
-        load_kernel,
-        out_shape=jax.ShapeDtypeStruct(conv5_weight.shape, BF),
-        in_specs=[HBM, VMEM],
-        out_specs=VMEM,
-        scratch_shapes=[pltpu.SemaphoreType.DMA],
-        cost_estimate=cost(flops=0, bytes_accessed=108 * f4 * f5),
-        compiler_params=PARAMS,
-        name="load_conv5_weight",
-    )(pltpu.with_memory_space_constraint(conv5_weight, pltpu.HBM), pack)
     by_y = swap(pack, 2)
     by_z = swap(pack, 1)
     by_both = swap(pack, 3)
     gy, gz = 2 * ny // 2, 2 * nz // 2
     own, other = pl.pallas_call(
         functools.partial(finish_kernel, ny=ny, nz=nz, planes=planes),
-        out_shape=(jax.ShapeDtypeStruct((gy * gz, f5), F32), jax.ShapeDtypeStruct((gy * gz, f5), F32)),
+        out_shape=(jax.ShapeDtypeStruct((gy * gz, f5), F32), jax.ShapeDtypeStruct((gy * gz, f5), BF)),
         in_specs=[VMEM] * 5,
         out_specs=(VMEM, VMEM),
         scratch_shapes=[
@@ -362,7 +346,7 @@
         cost_estimate=cost(flops=4 * gy * gz * 9 * f4 * f5, bytes_accessed=36 * f4 * f5),
         compiler_params=PARAMS,
         name="finish_and_conv5",
-    )(pack, by_y, by_z, by_both, kernel5)
+    )(pack, by_y, by_z, by_both, conv5_weight)
     features = pl.pallas_call(
         add_kernel,
         out_shape=jax.ShapeDtypeStruct((gy * gz, f5), BF),

time: 15.6 us -> 15.5 us (level)
  Pallas kernels: 5.68 us -> 4.2 us
  waiting for transfers between devices: 5.03 us -> 6.42 us
    pallas_call x1 -> x0, Pallas kernels: 1.48 us -> none  [pair_body(): pl.pallas_call(load_kernel, out_shape=jax.ShapeDtypeStruct(conv5_weight.s...]
    ppermute x5, waiting for transfers between devices: 5.03 us -> 6.42 us  [swap(): return lax.ppermute(x, GROUP, [(i, i ^ flips) for i in range(8)])]
  transfers between devices with their start and end apart: 5 -> 5, of which waited for: 4 -> 4; matrix products, arithmetic and copies ran while one was open for 0% -> 0% of each run, Pallas kernels for 20% -> 10%
where the time goes in v4:
time: 15.5 us; the launch traced here: 15.4 us
  waiting for transfers between devices  6.42 us (41%)
  starting transfers between devices  4.67 us (30%)
  Pallas kernels  4.2 us (27%)
    ppermute x5, waiting for transfers between devices, swap(): return lax.ppermute(x, GROUP, [(i, i ^ flips) for i in range(8)])  6.42 us
    ppermute x5, starting transfers between devices, swap(): return lax.ppermute(x, GROUP, [(i, i ^ flips) for i in range(8)])  4.67 us
    pallas_call x1, Pallas kernels, pair_body(): pl.pallas_call(prepare_kernel, out_shape=(jax.ShapeDtypeStruct((3, planes...  1.57 us
    pallas_call x1, Pallas kernels, pair_body(): pl.pallas_call(pack_kernel, out_shape=jax.ShapeDtypeStruct((packed, f4),...  1.38 us
    pallas_call x1, Pallas kernels, pair_body(): pl.pallas_call(add_kernel, out_shape=jax.ShapeDtypeStruct((gy * gz, f5),...  0.64 us
    pallas_call x1, Pallas kernels, pair_body(): pl.pallas_call(functools.partial(finish_kernel, ny=ny, nz=nz, planes=plan...  0.61 us
  transfers between devices with their start and end apart: 5, of which 4 were waited for; matrix products, arithmetic and copies ran while one was open for 0% of the time, Pallas kernels for 10%

profile of v4, /device:TPU:0, one launch (start us, length us, event | category | flops | bytes accessed | tf_op | source)
XLA Modules:
  0.0 15.4 jit_solution(9044938905159398255)
XLA Ops:
  0.0 0.5 %collective-permute-start = (bf16[2,16,16,128]{3,2,1,0:T(8,128)(2,1)}, bf16[2,16,16,128]{3,2,1,0:T(8,128)(2,1)S(1)}, u32[]{:S(2)}, u32[]{:S(2)}) collective-permute-start(bf16[2,16,16,128]{3,2,1,0:T(8,128)(2,1)} %v_hbm.1), channel_id=1, source_target_pairs={{0,4},{1,5},{2,6},{3,7},{4,0},{5,1},{6,2},{7,3},{8,12},{9,13},{10,... | collective-permute-start | bytes 393224 | tf_op jit(solution)/shard_map/ppermute | solution.py:287
  0.5 1.6 %prepare.1 = (bf16[3,2,20,16,128]{4,3,2,1,0:T(8,128)(2,1)S(1)}, bf16[2,24,384]{2,1,0:T(8,128)(2,1)S(1)}, bf16[3,3,3,128,256]{4,3,2,1,0:T(8,128)(2,1)S(1)}) custom-call(bf16[2,16,16,128]{3,2,1,0:T(8,128)(2,1)} %v_hbm.1, bf16[3,3,3,128,256]{4,3,2,1,0:T(8,128)(2,1)} %w_hbm.1), custom_call_target="tpu_custom_call" | custom-call | flops 1310720 | bytes 786432 | tf_op jit(solution)/shard_map/prepare/pallas_call | solution.py:292
  2.0 0.0 copy-start
  2.0 0.0 collective-permute-done.r_ref
  2.1 1.4 %conv4_pool_pack.1.q0 = bf16[192,256]{1,0:T(8,128)(2,1)S(1)} custom-call(bf16[2,16,16,128]{3,2,1,0:T(8,128)(2,1)S(1)} %collective-permute-done.r_ref, bf16[3,3,3,128,256]{4,3,2,1,0:T(8,128)(2,1)S(1)} %get-tuple-element.10.w_ref, bf16[3,2,20,16,128]{4,3,2,1,0:T(8,128)(2,1)S(1)} %get-tuple-element.11.own_ref, bf16[2,24,384]{2,1,0:T(8,128)(2,1)S(1)} %get-tuple-element.12.edge_ref), custom_call_target="tpu_custom_call" | custom-call | flops 802160640 | bytes 1769472 | tf_op jit(solution)/shard_map/conv4_pool_pack/pallas_call | solution.py:314
  3.4 3.5 %collective-permute-start.3 = (bf16[192,256]{1,0:T(8,128)(2,1)S(1)}, bf16[192,256]{1,0:T(8,128)(2,1)S(1)}, u32[]{:S(2)}, u32[]{:S(2)}) collective-permute-start(bf16[192,256]{1,0:T(8,128)(2,1)S(1)} %conv4_pool_pack.1.q0), channel_id=1, source_target_pairs={{0,3},{1,2},{2,1},{3,0},{4,7},{5,6},{6,5},{7,4},{8,11},{9,10},{10,... | collective-permute-start | bytes 294920 | tf_op jit(solution)/shard_map/ppermute | solution.py:287
  6.9 0.5 %collective-permute-start.2 = (bf16[192,256]{1,0:T(8,128)(2,1)S(1)}, bf16[192,256]{1,0:T(8,128)(2,1)S(1)}, u32[]{:S(2)}, u32[]{:S(2)}) collective-permute-start(bf16[192,256]{1,0:T(8,128)(2,1)S(1)} %conv4_pool_pack.1.q0), channel_id=1, source_target_pairs={{0,1},{1,0},{2,3},{3,2},{4,5},{5,4},{6,7},{7,6},{8,9},{9,8},{10,11... | collective-permute-start | bytes 294920 | tf_op jit(solution)/shard_map/ppermute | solution.py:287
  7.5 0.1 collective-permute-start.1
  7.6 2.9 %collective-permute-done.3.q3 = bf16[192,256]{1,0:T(8,128)(2,1)S(1)} collective-permute-done((bf16[192,256]{1,0:T(8,128)(2,1)S(1)}, bf16[192,256]{1,0:T(8,128)(2,1)S(1)}, u32[]{:S(2)}, u32[]{:S(2)}) %collective-permute-start.3) | collective-permute-done | bytes 98336 | tf_op jit(solution)/shard_map/ppermute | solution.py:287
  10.5 2.0 %collective-permute-done.2.q2 = bf16[192,256]{1,0:T(8,128)(2,1)S(1)} collective-permute-done((bf16[192,256]{1,0:T(8,128)(2,1)S(1)}, bf16[192,256]{1,0:T(8,128)(2,1)S(1)}, u32[]{:S(2)}, u32[]{:S(2)}) %collective-permute-start.2) | collective-permute-done | bytes 98336 | tf_op jit(solution)/shard_map/ppermute | solution.py:287
  12.5 0.2 %collective-permute-done.1.q1 = bf16[192,256]{1,0:T(8,128)(2,1)S(1)} collective-permute-done((bf16[192,256]{1,0:T(8,128)(2,1)S(1)}, bf16[192,256]{1,0:T(8,128)(2,1)S(1)}, u32[]{:S(2)}, u32[]{:S(2)}) %collective-permute-start.1) | collective-permute-done | bytes 98336 | tf_op jit(solution)/shard_map/ppermute | solution.py:287
  12.8 0.0 copy-done
  12.8 0.6 %finish_and_conv5.1 = (f32[256,128]{1,0:T(8,128)S(1)}, bf16[256,128]{1,0:T(8,128)(2,1)S(1)}) custom-call(bf16[192,256]{1,0:T(8,128)(2,1)S(1)} %conv4_pool_pack.1.q0, bf16[192,256]{1,0:T(8,128)(2,1)S(1)} %collective-permute-done.1.q1, bf16[192,256]{1,0:T(8,128)(2,1)S(1)} %collective-permute-done.2.q2, bf16[192,256]{1,0:T(8,128)(2,1)S(1)} %collective-permute-done.3.q3, ...), custom_call_target="tpu_custom_call" | custom-call | flops 301989888 | bytes 1179648 | tf_op jit(solution)/shard_map/finish_and_conv5/pallas_call | solution.py:335
  13.4 0.1 collective-permute-start.4
  13.5 1.2 %collective-permute-done.4.other_ref = bf16[256,128]{1,0:T(8,128)(2,1)S(1)} collective-permute-done((bf16[256,128]{1,0:T(8,128)(2,1)S(1)}, bf16[256,128]{1,0:T(8,128)(2,1)S(1)}, u32[]{:S(2)}, u32[]{:S(2)}) %collective-permute-start.4) | collective-permute-done | bytes 65568 | tf_op jit(solution)/shard_map/ppermute | solution.py:287
  14.7 0.6 %add_planes.1 = bf16[256,128]{1,0:T(8,128)(2,1)} custom-call(f32[256,128]{1,0:T(8,128)S(1)} %get-tuple-element.13.own_ref, bf16[256,128]{1,0:T(8,128)(2,1)S(1)} %collective-permute-done.4.other_ref), custom_call_target="tpu_custom_call" | custom-call | tf_op jit(solution)/shard_map/add_planes/pallas_call | solution.py:350
Async XLA Ops:
  0.0 2.0 %collective-permute-start = (bf16[2,16,16,128]{3,2,1,0:T(8,128)(2,1)}, bf16[2,16,16,128]{3,2,1,0:T(8,128)(2,1)S(1)}, u32[]{:S(2)}, u32[]{:S(2)}) collective-permute-start(bf16[2,16,16,128]{3,2,1,0:T(8,128)(2,1)} %v_hbm.1), channel_id=1, source_target_pairs={{0,4},{1,5},{2,6},{3,7},{4,0},{5,1},{6,2},{7,3},{8,12},{9,13},{10,... | collective-permute-start | bytes 393224 | tf_op jit(solution)/shard_map/ppermute | solution.py:287
  2.0 10.7 %copy-start = (bf16[3,3,3,256,128]{4,3,2,1,0:T(8,128)(2,1)S(1)}, bf16[3,3,3,256,128]{4,3,2,1,0:T(8,128)(2,1)}, u32[]{:S(2)}) copy-start(bf16[3,3,3,256,128]{4,3,2,1,0:T(8,128)(2,1)} %w_ref.1) | copy-start | bytes 5308420
  3.4 7.0 %collective-permute-start.3 = (bf16[192,256]{1,0:T(8,128)(2,1)S(1)}, bf16[192,256]{1,0:T(8,128)(2,1)S(1)}, u32[]{:S(2)}, u32[]{:S(2)}) collective-permute-start(bf16[192,256]{1,0:T(8,128)(2,1)S(1)} %conv4_pool_pack.1.q0), channel_id=1, source_target_pairs={{0,3},{1,2},{2,1},{3,0},{4,7},{5,6},{6,5},{7,4},{8,11},{9,10},{10,... | collective-permute-start | bytes 294920 | tf_op jit(solution)/shard_map/ppermute | solution.py:287
  6.9 5.6 %collective-permute-start.2 = (bf16[192,256]{1,0:T(8,128)(2,1)S(1)}, bf16[192,256]{1,0:T(8,128)(2,1)S(1)}, u32[]{:S(2)}, u32[]{:S(2)}) collective-permute-start(bf16[192,256]{1,0:T(8,128)(2,1)S(1)} %conv4_pool_pack.1.q0), channel_id=1, source_target_pairs={{0,1},{1,0},{2,3},{3,2},{4,5},{5,4},{6,7},{7,6},{8,9},{9,8},{10,11... | collective-permute-start | bytes 294920 | tf_op jit(solution)/shard_map/ppermute | solution.py:287
  7.5 5.3 %collective-permute-start.1 = (bf16[192,256]{1,0:T(8,128)(2,1)S(1)}, bf16[192,256]{1,0:T(8,128)(2,1)S(1)}, u32[]{:S(2)}, u32[]{:S(2)}) collective-permute-start(bf16[192,256]{1,0:T(8,128)(2,1)S(1)} %conv4_pool_pack.1.q0), channel_id=1, source_target_pairs={{0,2},{1,3},{2,0},{3,1},{4,6},{5,7},{6,4},{7,5},{8,10},{9,11},{10,... | collective-permute-start | bytes 294920 | tf_op jit(solution)/shard_map/ppermute | solution.py:287
  13.4 1.3 %collective-permute-start.4 = (bf16[256,128]{1,0:T(8,128)(2,1)S(1)}, bf16[256,128]{1,0:T(8,128)(2,1)S(1)}, u32[]{:S(2)}, u32[]{:S(2)}) collective-permute-start(bf16[256,128]{1,0:T(8,128)(2,1)S(1)} %get-tuple-element.14), channel_id=1, source_target_pairs={{0,4},{1,5},{2,6},{3,7},{4,0},{5,1},{6,2},{7,3},{8,12},{9,13},{10,... | collective-permute-start | bytes 196616 | tf_op jit(solution)/shard_map/ppermute | solution.py:287

commit v5 on v0

--- a/solution.py
+++ b/solution.py
@@ -1,7 +1,18 @@
+import functools
+
 import jax
 import jax.numpy as jnp
 from jax import lax
+from jax.experimental import pallas as pl
+from jax.experimental.pallas import tpu as pltpu
 from jax.sharding import PartitionSpec as P
+
+BF = jnp.bfloat16
+F32 = jnp.float32
+VMEM = pl.BlockSpec(memory_space=pltpu.VMEM)
+HBM = pl.BlockSpec(memory_space=pltpu.HBM)
+GROUP = ("gx", "gy", "gz")
+PARAMS = pltpu.CompilerParams(vmem_limit_bytes=8 * 2**20)
 
 
 def extended(cells, sides, width):
@@ -50,7 +61,7 @@
     return jnp.max(blocks, axis=(1, 3, 5)).astype(jnp.bfloat16)
 
 
-def body(volume, conv4_weight, conv5_weight):
+def general_body(volume, conv4_weight, conv5_weight):
     padded = extended(volume, (("gx", 0), ("gy", 1), ("gz", 2)), 1)
     pooled = pool_leaky(conv_local(padded, conv4_weight))
     strips = lax.all_gather(pooled, "gz", axis=2, tiled=True)
@@ -58,6 +69,281 @@
     bordered = extended(slab, (("gx", 0),), 1)
     bordered = jnp.pad(bordered, ((0, 0), (1, 1), (1, 1), (0, 0)))
     return conv_local(bordered, conv5_weight).astype(jnp.bfloat16)
+
+
+def leaky(v):
+    return jnp.where(v > 0, v, 0.3 * v)
+
+
+def shifted_copies(plane, out_ref, index, border):
+    ny, nz, nc = plane.shape
+    flat = plane.reshape(ny * nz, nc).astype(F32)
+    at = lax.broadcasted_iota(jnp.int32, flat.shape, 0) % nz
+    after = jnp.where(at == 0, 0.0, pltpu.roll(flat, 1, 0))
+    before = jnp.where(at == nz - 1, 0.0, pltpu.roll(flat, ny * nz - 1, 0))
+    for dz, moved in enumerate((after, flat, before)):
+        if border:
+            out_ref[dz, index, 0:border] = jnp.zeros((border, nz, nc), BF)
+            out_ref[dz, index, border + ny : 2 * border + ny] = jnp.zeros((border, nz, nc), BF)
+        out_ref[dz, index, border : border + ny] = moved.astype(BF).reshape(ny, nz, nc)
+
+
+def windows(shift_ref, index, first, count):
+    nz, nc = shift_ref.shape[3:]
+    parts = []
+    for dy in range(3):
+        for dz in range(3):
+            parts.append(shift_ref[dz, index, first + dy : first + dy + count].reshape(count * nz, nc))
+    return jnp.concatenate(parts, axis=1)
+
+
+def edge_columns(plane, flat_ref, at_z):
+    ny, nz, nc = plane.shape
+    flat_ref[...] = plane.reshape(ny * nz, nc).astype(F32)
+    low = [flat_ref[pl.ds(z, ny, nz), :] for z in (0, 1)]
+    high = [flat_ref[pl.ds(z, ny, nz), :] for z in (nz - 2, nz - 1)]
+    return jnp.where(at_z == 0, jnp.concatenate(high, axis=1), jnp.concatenate(low, axis=1)).astype(BF)
+
+
+def prepare_kernel(v_hbm, w_hbm, shift_ref, column_ref, w_ref, v_ref, flat_ref, v_sem, w_sem):
+    load_v = pltpu.make_async_copy(v_hbm, v_ref, v_sem)
+    load_w = pltpu.make_async_copy(w_hbm, w_ref, w_sem)
+    load_v.start()
+    load_w.start()
+    at_z = lax.axis_index("gz")
+    load_v.wait()
+    for p in range(v_ref.shape[0]):
+        shifted_copies(v_ref[p], shift_ref, p, 1)
+        column_ref[p] = edge_columns(v_ref[p], flat_ref, at_z)
+    load_w.wait()
+
+
+def pack_kernel(r_ref, w_ref, own_ref, column_ref, out_ref, h_ref, shift_ref, flat_ref, pair_ref):
+    at_x, at_y, at_z = (lax.axis_index(axis) for axis in GROUP)
+    planes, ny, nz, nc = r_ref.shape
+    filters = w_ref.shape[4]
+    rows = ny * nz
+    plane = r_ref[at_x]
+    mine = 1 - at_x
+    shifted_copies(plane, shift_ref, 0, 1)
+    cells = ny * nz // 4
+    columns = cells + (planes + 1) * nz
+    first_row = (ny - 2) * (1 - at_y) + 1
+
+    def put_edges(slot, source_ref, index, column):
+        begin = pl.multiple_of(cells + slot * nz, 16)
+        near = [source_ref[1, index, first_row + side] for side in range(2)]
+        out_ref[pl.ds(begin, nz)] = jnp.concatenate(near, axis=1)
+        begin = pl.multiple_of(columns + slot * ny, 16)
+        out_ref[pl.ds(begin, ny)] = column
+
+    put_edges(2 * mine, shift_ref, 0, edge_columns(plane, flat_ref, at_z))
+    for p in range(planes):
+        put_edges(at_x + p, own_ref, p, column_ref[p])
+    step = 8
+    for first in range(0, ny, step):
+        lhs = jnp.concatenate([windows(own_ref, source, first, step) for source in range(planes)], axis=1)
+        halo = windows(shift_ref, 0, first, step)
+        sums = jnp.dot(lhs, w_ref[pl.ds(at_x, planes)].reshape(planes * 9 * nc, filters), preferred_element_type=F32)
+        sums += jnp.dot(halo, w_ref[2 * mine].reshape(9 * nc, filters), preferred_element_type=F32)
+        rest = w_ref[pl.ds(mine, planes)].reshape(planes * 9 * nc, filters)
+        h_ref[first * nz : (first + step) * nz] = jnp.maximum(sums, jnp.dot(lhs, rest, preferred_element_type=F32))
+
+    def row(y):
+        return h_ref[y * nz : (y + 1) * nz]
+
+    low = -jnp.inf
+    is_edge = lax.broadcasted_iota(jnp.int32, (nz, filters), 0) == (nz - 1) * (1 - at_z)
+    for k in range(ny // 2):
+        first, second = row(2 * k), row(2 * k + 1)
+        if k == 0:
+            first = jnp.where(at_y == 1, low, first)
+        if k == ny // 2 - 1:
+            second = jnp.where(at_y == 0, low, second)
+        both = jnp.where(is_edge, low, jnp.maximum(first, second))
+        for half in range(filters // 128):
+            pair_ref[half, k * nz : (k + 1) * nz] = both[:, half * 128 : (half + 1) * 128]
+    pooled = [
+        jnp.maximum(pair_ref[half, pl.ds(0, cells, 2), :], pair_ref[half, pl.ds(1, cells, 2), :])
+        for half in range(filters // 128)
+    ]
+    out_ref[0:cells] = leaky(jnp.concatenate(pooled, axis=1)).astype(out_ref.dtype)
+
+
+def finish_kernel(
+    q0, q1, q2, q3, w4_ref, w_ref, own_ref, other_ref, pack_ref, cross_ref, h_ref, full_ref, pair_ref, shift_ref, *, ny, nz, planes
+):
+    at_x, at_y, at_z = (lax.axis_index(axis) for axis in GROUP)
+    mine = 1 - at_x
+    filters = w_ref.shape[3]
+    outs = w_ref.shape[4]
+    nc = w4_ref.shape[3]
+    here = 2 * at_y + at_z
+    pack_ref[here] = q0[...]
+    pack_ref[2 * (1 - at_y) + at_z] = q1[...]
+    pack_ref[2 * at_y + 1 - at_z] = q2[...]
+    pack_ref[2 * (1 - at_y) + 1 - at_z] = q3[...]
+    py, pz = ny // 2, nz // 2
+    cells = py * pz
+    columns = cells + (planes + 1) * nz
+
+    for slot in range(planes + 1):
+        lines = []
+        for side in range(4):
+            lanes = slice(side % 2 * nc, side % 2 * nc + nc)
+            begin = cells + slot * nz
+            parts = [pack_ref[2 * (side // 2) + qz, begin : begin + nz, lanes] for qz in range(2)]
+            lines.append(jnp.concatenate(parts, axis=0)[None])
+        shifted_copies(jnp.concatenate(lines, axis=0), cross_ref.at[0], slot, 0)
+        lines = []
+        for side in range(4):
+            lanes = slice(side % 2 * nc, side % 2 * nc + nc)
+            begin = columns + slot * ny
+            parts = [pack_ref[2 * qy + side // 2, begin : begin + ny, lanes] for qy in range(2)]
+            lines.append(jnp.concatenate(parts, axis=0)[None])
+        shifted_copies(jnp.concatenate(lines, axis=0), cross_ref.at[1], slot, 0)
+
+    def cross_windows(kind, slot):
+        parts = []
+        for dy in range(3):
+            for dz in range(3):
+                along, over = (dz, dy) if kind == 0 else (dy, dz)
+                part = cross_ref[kind, along, slot, over : over + 2]
+                parts.append(part.reshape(part.shape[0] * part.shape[1], nc))
+        return jnp.concatenate(parts, axis=1)
+
+    wins = [jnp.concatenate([cross_windows(kind, slot) for kind in range(2)], axis=0) for slot in range(planes + 1)]
+    rhs = w4_ref[...].reshape((planes + 1) * 9 * nc, filters)
+    inner = jnp.dot(jnp.concatenate(wins, axis=1), rhs, preferred_element_type=F32)
+    wins = [
+        jnp.concatenate([cross_windows(kind, at_x + p) for kind in range(2)], axis=0) for p in range(planes)
+    ]
+    rhs = w4_ref[pl.ds(mine, planes)].reshape(planes * 9 * nc, filters)
+    h_ref[...] = jnp.maximum(inner, jnp.dot(jnp.concatenate(wins, axis=1), rhs, preferred_element_type=F32))
+
+    def halve(v, slot):
+        parts = []
+        for half in range(filters // 128):
+            pair_ref[slot, half] = v[:, half * 128 : (half + 1) * 128]
+            count = v.shape[0] // 2
+            parts.append(
+                jnp.maximum(pair_ref[slot, half, pl.ds(0, count, 2), :], pair_ref[slot, half, pl.ds(1, count, 2), :])
+            )
+        return jnp.concatenate(parts, axis=1)
+
+    for qy in range(2):
+        for qz in range(2):
+            pooled = pack_ref[2 * qy + qz, 0:cells].astype(F32)
+            full_ref[qy * py : (qy + 1) * py, qz * pz : (qz + 1) * pz] = pooled.reshape(py, pz, filters)
+    pooled = full_ref[...]
+    at_row = lax.broadcasted_iota(jnp.int32, (2 * py, 1, filters), 0)
+    at_col = lax.broadcasted_iota(jnp.int32, (1, 2 * pz, filters), 1)
+    for side in range(2):
+        first = side * 2 * nz
+        line = h_ref[first : first + 2 * nz]
+        line = leaky(halve(line, side))
+        pooled = jnp.maximum(pooled, jnp.where(at_row == py - 1 + side, line[None], -jnp.inf))
+        first = 4 * nz + side * 2 * ny
+        line = h_ref[first : first + 2 * ny]
+        line = leaky(halve(line, 2 + side))
+        pooled = jnp.maximum(pooled, jnp.where(at_col == pz - 1 + side, line[:, None, :], -jnp.inf))
+    shifted_copies(pooled.astype(BF), shift_ref, 0, 1)
+    rhs = jnp.concatenate(
+        [w_ref[1].reshape(9 * filters, outs), w_ref[2 * at_x].reshape(9 * filters, outs)], axis=1
+    )
+    step = 8
+    for first in range(0, ny, step):
+        sums = jnp.dot(windows(shift_ref, 0, first, step), rhs, preferred_element_type=F32)
+        own_ref[first * nz : (first + step) * nz] = sums[:, :outs]
+        other_ref[first * nz : (first + step) * nz] = sums[:, outs:].astype(other_ref.dtype)
+
+
+def add_kernel(own_ref, other_ref, out_ref):
+    out_ref[...] = (own_ref[...] + other_ref[...]).astype(out_ref.dtype)
+
+
+def pair_body(volume, conv4_weight, conv5_weight):
+    planes, ny, nz, nc = volume.shape
+    f4, f5 = conv4_weight.shape[4], conv5_weight.shape[4]
+
+    def swap(x, flips):
+        return lax.ppermute(x, GROUP, [(i, i ^ flips) for i in range(8)])
+
+    cost = functools.partial(pl.CostEstimate, transcendentals=0)
+    rows = ny * nz
+    theirs = swap(volume, 4)
+    moved, columns, kernel4 = pl.pallas_call(
+        prepare_kernel,
+        out_shape=(
+            jax.ShapeDtypeStruct((3, planes, ny + 2, nz, nc), BF),
+            jax.ShapeDtypeStruct((planes, ny, 2 * nc), BF),
+            jax.ShapeDtypeStruct(conv4_weight.shape, BF),
+        ),
+        in_specs=[HBM, HBM],
+        out_specs=(VMEM, VMEM, VMEM),
+        scratch_shapes=[
+            pltpu.VMEM(volume.shape, BF),
+            pltpu.VMEM((rows, nc), F32),
+            pltpu.SemaphoreType.DMA,
+            pltpu.SemaphoreType.DMA,
+        ],
+        cost_estimate=cost(flops=20 * planes * rows * nc, bytes_accessed=54 * nc * f4),
+        compiler_params=PARAMS,
+        name="prepare",
+    )(*(pltpu.with_memory_space_constraint(x, pltpu.HBM) for x in (volume, conv4_weight)))
+    packed = rows // 4 + (planes + 1) * (ny + nz)
+    pack = pl.pallas_call(
+        pack_kernel,
+        out_shape=jax.ShapeDtypeStruct((packed, f4), BF),
+        in_specs=[VMEM] * 4,
+        out_specs=VMEM,
+        scratch_shapes=[
+            pltpu.VMEM((rows, f4), F32),
+            pltpu.VMEM((3, 1, ny + 2, nz, nc), BF),
+            pltpu.VMEM((rows, nc), F32),
+            pltpu.VMEM((f4 // 128, rows // 2, 128), F32),
+        ],
+        cost_estimate=cost(flops=5 * 2 * rows * 9 * nc * f4, bytes_accessed=54 * nc * f4),
+        compiler_params=PARAMS,
+        name="conv4_pool_pack",
+    )(theirs, kernel4, moved, columns)
+    by_y = swap(pack, 2)
+    by_z = swap(pack, 1)
+    by_both = swap(pack, 3)
+    gy, gz = 2 * ny // 2, 2 * nz // 2
+    own, other = pl.pallas_call(
+        functools.partial(finish_kernel, ny=ny, nz=nz, planes=planes),
+        out_shape=(jax.ShapeDtypeStruct((gy * gz, f5), F32), jax.ShapeDtypeStruct((gy * gz, f5), BF)),
+        in_specs=[VMEM] * 6,
+        out_specs=(VMEM, VMEM),
+        scratch_shapes=[
+            pltpu.VMEM((4, packed, f4), BF),
+            pltpu.VMEM((2, 3, planes + 1, 4, 2 * nz, nc), BF),
+            pltpu.VMEM((4 * ny + 4 * nz, f4), F32),
+            pltpu.VMEM((gy, gz, f4), F32),
+            pltpu.VMEM((4, f4 // 128, 2 * nz, 128), F32),
+            pltpu.VMEM((3, 1, gy + 2, gz, f4), BF),
+        ],
+        cost_estimate=cost(flops=4 * gy * gz * 9 * f4 * f5, bytes_accessed=36 * f4 * f5),
+        compiler_params=PARAMS,
+        name="finish_and_conv5",
+    )(pack, by_y, by_z, by_both, kernel4, conv5_weight)
+    features = pl.pallas_call(
+        add_kernel,
+        out_shape=jax.ShapeDtypeStruct((gy * gz, f5), BF),
+        in_specs=[VMEM] * 2,
+        out_specs=VMEM,
+        compiler_params=PARAMS,
+        name="add_planes",
+    )(own, swap(other, 4))
+    return features.reshape(1, gy, gz, f5)
+
+
+def body(volume, conv4_weight, conv5_weight):
+    paired = all(lax.axis_size(axis) == 2 for axis in GROUP)
+    if paired and volume.shape[0] == 2 and volume.shape[1] == volume.shape[2] and conv4_weight.shape[4] == 2 * conv4_weight.shape[3]:
+        return pair_body(volume, conv4_weight, conv5_weight)
+    return general_body(volume, conv4_weight, conv5_weight)
 
 
 def solution(mesh):

time: 55.7 us -> 15 us (0.27)
  starting transfers between devices: 16.5 us -> 4.67 us
  matrix products: 10.8 us -> 0 us
  blocking collectives: 9.52 us -> 0 us
  waiting for transfers between devices: 12.4 us -> 5.72 us
  Pallas kernels: 0 us -> 4.37 us
  local copies, waits for them, and re-layouts: 3.45 us -> 0.01 us
  other arithmetic: 2.17 us -> 0 us
    ppermute x8 -> x5, starting transfers between devices: 16.5 us -> 4.67 us  [swap(): return lax.ppermute(x, GROUP, [(i, i ^ flips) for i in range(8)])]
    dot_general x54 -> x0, matrix products: 10.8 us -> none  [conv_local(): jnp.dot(window, kernel[along_x, along_y, along_z], preferred_element_type...]
    all_gather x2 -> x0, blocking collectives: 9.52 us -> none  [the longest x1 4.93 us: body(): slab = lax.all_gather(strips, 'gy', axis=1, tiled=True)]
    ppermute x8 -> x5, waiting for transfers between devices: 12.4 us -> 5.72 us  [swap(): return lax.ppermute(x, GROUP, [(i, i ^ flips) for i in range(8)])]
    pallas_call x0 -> x4, Pallas kernels: none -> 4.37 us  [the longest x1 1.57 us: pair_body(): pl.pallas_call(prepare_kernel, out_shape=(jax.ShapeDtypeStruct((3, planes...]
    slice x5 -> x0, local copies, waits for them, and re-layouts: 1.72 us -> none  [the longest x1 1.01 us: extended(): head = lax.slice_in_dim(cells, 0, width, axis=dim)]
    concatenate x4 -> x0, other arithmetic: 1.66 us -> none  [extended(): jnp.concatenate([lax.ppermute(tail, axis, [(i, (i + 1) % count) for i in...]
    unnamed x7 -> x2, local copies, waits for them, and re-layouts: 1.41 us -> 0.01 us
  transfers between devices with their start and end apart: 8 -> 5, of which waited for: 5 -> 4; matrix products, arithmetic and copies ran while one was open for 0% -> 0% of each run, Pallas kernels for 0% -> 11%
where the time goes in v5:
time: 15 us; the launch traced here: 14.8 us
  waiting for transfers between devices  5.72 us (38%)
  starting transfers between devices  4.67 us (31%)
  Pallas kernels  4.37 us (29%)
    ppermute x5, waiting for transfers between devices, swap(): return lax.ppermute(x, GROUP, [(i, i ^ flips) for i in range(8)])  5.72 us
    ppermute x5, starting transfers between devices, swap(): return lax.ppermute(x, GROUP, [(i, i ^ flips) for i in range(8)])  4.67 us
    pallas_call x1, Pallas kernels, pair_body(): pl.pallas_call(prepare_kernel, out_shape=(jax.ShapeDtypeStruct((3, planes...  1.57 us
    pallas_call x1, Pallas kernels, pair_body(): pl.pallas_call(functools.partial(finish_kernel, ny=ny, nz=nz, planes=plan...  1.17 us
    pallas_call x1, Pallas kernels, pair_body(): pl.pallas_call(pack_kernel, out_shape=jax.ShapeDtypeStruct((packed, f4),...  0.99 us
    pallas_call x1, Pallas kernels, pair_body(): pl.pallas_call(add_kernel, out_shape=jax.ShapeDtypeStruct((gy * gz, f5),...  0.64 us
  transfers between devices with their start and end apart: 5, of which 4 were waited for; matrix products, arithmetic and copies ran while one was open for 0% of the time, Pallas kernels for 11%

profile of v5, /device:TPU:0, one launch (start us, length us, event | category | flops | bytes accessed | tf_op | source)
XLA Modules:
  0.0 14.8 jit_solution(14785296524627855520)
XLA Ops:
  0.0 0.5 %collective-permute-start = (bf16[2,16,16,128]{3,2,1,0:T(8,128)(2,1)}, bf16[2,16,16,128]{3,2,1,0:T(8,128)(2,1)S(1)}, u32[]{:S(2)}, u32[]{:S(2)}) collective-permute-start(bf16[2,16,16,128]{3,2,1,0:T(8,128)(2,1)} %v_hbm.1), channel_id=1, source_target_pairs={{0,4},{1,5},{2,6},{3,7},{4,0},{5,1},{6,2},{7,3},{8,12},{9,13},{10,... | collective-permute-start | bytes 393224 | tf_op jit(solution)/shard_map/ppermute | solution.py:270
  0.5 1.6 %prepare.1 = (bf16[3,2,18,16,128]{4,3,2,1,0:T(8,128)(2,1)S(1)}, bf16[2,16,256]{2,1,0:T(8,128)(2,1)S(1)}, bf16[3,3,3,128,256]{4,3,2,1,0:T(8,128)(2,1)S(1)}) custom-call(bf16[2,16,16,128]{3,2,1,0:T(8,128)(2,1)} %v_hbm.1, bf16[3,3,3,128,256]{4,3,2,1,0:T(8,128)(2,1)} %w_hbm.1), custom_call_target="tpu_custom_call" | custom-call | flops 1310720 | bytes 1769472 | tf_op jit(solution)/shard_map/prepare/pallas_call | solution.py:275
  2.0 0.0 copy-start
  2.0 0.0 collective-permute-done.r_ref
  2.1 1.0 %conv4_pool_pack.1.q0 = bf16[160,256]{1,0:T(8,128)(2,1)S(1)} custom-call(bf16[2,16,16,128]{3,2,1,0:T(8,128)(2,1)S(1)} %collective-permute-done.r_ref, bf16[3,3,3,128,256]{4,3,2,1,0:T(8,128)(2,1)S(1)} %get-tuple-element.10.w_ref.w4_ref, bf16[3,2,18,16,128]{4,3,2,1,0:T(8,128)(2,1)S(1)} %get-tuple-element.11.own_ref, ...), custom_call_target="tpu_custom_call" | custom-call | flops 754974720 | bytes 1769472 | tf_op jit(solution)/shard_map/conv4_pool_pack/pallas_call | solution.py:295
  3.0 3.5 %collective-permute-start.3 = (bf16[160,256]{1,0:T(8,128)(2,1)S(1)}, bf16[160,256]{1,0:T(8,128)(2,1)S(1)}, u32[]{:S(2)}, u32[]{:S(2)}) collective-permute-start(bf16[160,256]{1,0:T(8,128)(2,1)S(1)} %conv4_pool_pack.1.q0), channel_id=1, source_target_pairs={{0,3},{1,2},{2,1},{3,0},{4,7},{5,6},{6,5},{7,4},{8,11},{9,10},{10,... | collective-permute-start | bytes 245768 | tf_op jit(solution)/shard_map/ppermute | solution.py:270
  6.6 0.5 %collective-permute-start.2 = (bf16[160,256]{1,0:T(8,128)(2,1)S(1)}, bf16[160,256]{1,0:T(8,128)(2,1)S(1)}, u32[]{:S(2)}, u32[]{:S(2)}) collective-permute-start(bf16[160,256]{1,0:T(8,128)(2,1)S(1)} %conv4_pool_pack.1.q0), channel_id=1, source_target_pairs={{0,1},{1,0},{2,3},{3,2},{4,5},{5,4},{6,7},{7,6},{8,9},{9,8},{10,11... | collective-permute-start | bytes 245768 | tf_op jit(solution)/shard_map/ppermute | solution.py:270
  7.1 0.1 collective-permute-start.1
  7.2 2.5 %collective-permute-done.3.q3 = bf16[160,256]{1,0:T(8,128)(2,1)S(1)} collective-permute-done((bf16[160,256]{1,0:T(8,128)(2,1)S(1)}, bf16[160,256]{1,0:T(8,128)(2,1)S(1)}, u32[]{:S(2)}, u32[]{:S(2)}) %collective-permute-start.3) | collective-permute-done | bytes 81952 | tf_op jit(solution)/shard_map/ppermute | solution.py:270
  9.7 1.7 %collective-permute-done.2.q2 = bf16[160,256]{1,0:T(8,128)(2,1)S(1)} collective-permute-done((bf16[160,256]{1,0:T(8,128)(2,1)S(1)}, bf16[160,256]{1,0:T(8,128)(2,1)S(1)}, u32[]{:S(2)}, u32[]{:S(2)}) %collective-permute-start.2) | collective-permute-done | bytes 81952 | tf_op jit(solution)/shard_map/ppermute | solution.py:270
  11.4 0.3 %collective-permute-done.1.q1 = bf16[160,256]{1,0:T(8,128)(2,1)S(1)} collective-permute-done((bf16[160,256]{1,0:T(8,128)(2,1)S(1)}, bf16[160,256]{1,0:T(8,128)(2,1)S(1)}, u32[]{:S(2)}, u32[]{:S(2)}) %collective-permute-start.1) | collective-permute-done | bytes 81952 | tf_op jit(solution)/shard_map/ppermute | solution.py:270
  11.7 0.0 copy-done
  11.7 1.2 %finish_and_conv5.1 = (f32[256,128]{1,0:T(8,128)S(1)}, bf16[256,128]{1,0:T(8,128)(2,1)S(1)}) custom-call(bf16[160,256]{1,0:T(8,128)(2,1)S(1)} %conv4_pool_pack.1.q0, bf16[160,256]{1,0:T(8,128)(2,1)S(1)} %collective-permute-done.1.q1, bf16[160,256]{1,0:T(8,128)(2,1)S(1)} %collective-permute-done.2.q2, bf16[160,256]{1,0:T(8,128)(2,1)S(1)} %collective-permute-done.3.q3, ...), custom_call_target="tpu_custom_call" | custom-call | flops 301989888 | bytes 1179648 | tf_op jit(solution)/shard_map/finish_and_conv5/pallas_call | solution.py:314
  12.9 0.1 collective-permute-start.4
  12.9 1.2 %collective-permute-done.4.other_ref = bf16[256,128]{1,0:T(8,128)(2,1)S(1)} collective-permute-done((bf16[256,128]{1,0:T(8,128)(2,1)S(1)}, bf16[256,128]{1,0:T(8,128)(2,1)S(1)}, u32[]{:S(2)}, u32[]{:S(2)}) %collective-permute-start.4) | collective-permute-done | bytes 65568 | tf_op jit(solution)/shard_map/ppermute | solution.py:270
  14.2 0.6 %add_planes.1 = bf16[256,128]{1,0:T(8,128)(2,1)} custom-call(f32[256,128]{1,0:T(8,128)S(1)} %get-tuple-element.13.own_ref, bf16[256,128]{1,0:T(8,128)(2,1)S(1)} %collective-permute-done.4.other_ref), custom_call_target="tpu_custom_call" | custom-call | tf_op jit(solution)/shard_map/add_planes/pallas_call | solution.py:331
Async XLA Ops:
  0.0 2.0 %collective-permute-start = (bf16[2,16,16,128]{3,2,1,0:T(8,128)(2,1)}, bf16[2,16,16,128]{3,2,1,0:T(8,128)(2,1)S(1)}, u32[]{:S(2)}, u32[]{:S(2)}) collective-permute-start(bf16[2,16,16,128]{3,2,1,0:T(8,128)(2,1)} %v_hbm.1), channel_id=1, source_target_pairs={{0,4},{1,5},{2,6},{3,7},{4,0},{5,1},{6,2},{7,3},{8,12},{9,13},{10,... | collective-permute-start | bytes 393224 | tf_op jit(solution)/shard_map/ppermute | solution.py:270
  2.0 9.7 %copy-start = (bf16[3,3,3,256,128]{4,3,2,1,0:T(8,128)(2,1)S(1)}, bf16[3,3,3,256,128]{4,3,2,1,0:T(8,128)(2,1)}, u32[]{:S(2)}) copy-start(bf16[3,3,3,256,128]{4,3,2,1,0:T(8,128)(2,1)} %w_ref.1) | copy-start | bytes 5308420
  3.0 6.7 %collective-permute-start.3 = (bf16[160,256]{1,0:T(8,128)(2,1)S(1)}, bf16[160,256]{1,0:T(8,128)(2,1)S(1)}, u32[]{:S(2)}, u32[]{:S(2)}) collective-permute-start(bf16[160,256]{1,0:T(8,128)(2,1)S(1)} %conv4_pool_pack.1.q0), channel_id=1, source_target_pairs={{0,3},{1,2},{2,1},{3,0},{4,7},{5,6},{6,5},{7,4},{8,11},{9,10},{10,... | collective-permute-start | bytes 245768 | tf_op jit(solution)/shard_map/ppermute | solution.py:270
  6.6 4.9 %collective-permute-start.2 = (bf16[160,256]{1,0:T(8,128)(2,1)S(1)}, bf16[160,256]{1,0:T(8,128)(2,1)S(1)}, u32[]{:S(2)}, u32[]{:S(2)}) collective-permute-start(bf16[160,256]{1,0:T(8,128)(2,1)S(1)} %conv4_pool_pack.1.q0), channel_id=1, source_target_pairs={{0,1},{1,0},{2,3},{3,2},{4,5},{5,4},{6,7},{7,6},{8,9},{9,8},{10,11... | collective-permute-start | bytes 245768 | tf_op jit(solution)/shard_map/ppermute | solution.py:270
  7.1 4.6 %collective-permute-start.1 = (bf16[160,256]{1,0:T(8,128)(2,1)S(1)}, bf16[160,256]{1,0:T(8,128)(2,1)S(1)}, u32[]{:S(2)}, u32[]{:S(2)}) collective-permute-start(bf16[160,256]{1,0:T(8,128)(2,1)S(1)} %conv4_pool_pack.1.q0), channel_id=1, source_target_pairs={{0,2},{1,3},{2,0},{3,1},{4,6},{5,7},{6,4},{7,5},{8,10},{9,11},{10,... | collective-permute-start | bytes 245768 | tf_op jit(solution)/shard_map/ppermute | solution.py:270
  12.9 1.3 %collective-permute-start.4 = (bf16[256,128]{1,0:T(8,128)(2,1)S(1)}, bf16[256,128]{1,0:T(8,128)(2,1)S(1)}, u32[]{:S(2)}, u32[]{:S(2)}) collective-permute-start(bf16[256,128]{1,0:T(8,128)(2,1)S(1)} %get-tuple-element.14), channel_id=1, source_target_pairs={{0,4},{1,5},{2,6},{3,7},{4,0},{5,1},{6,2},{7,3},{8,12},{9,13},{10,... | collective-permute-start | bytes 196616 | tf_op jit(solution)/shard_map/ppermute | solution.py:270

commit v6 on v5

--- a/solution.py
+++ b/solution.py
@@ -105,20 +105,32 @@
     return jnp.where(at_z == 0, jnp.concatenate(high, axis=1), jnp.concatenate(low, axis=1)).astype(BF)
 
 
-def prepare_kernel(v_hbm, w_hbm, shift_ref, column_ref, w_ref, v_ref, flat_ref, v_sem, w_sem):
+def prepare_kernel(v_hbm, w_hbm, shift_ref, column_ref, sum_ref, w_ref, v_ref, flat_ref, v_sem, w_sem):
     load_v = pltpu.make_async_copy(v_hbm, v_ref, v_sem)
-    load_w = pltpu.make_async_copy(w_hbm, w_ref, w_sem)
+    loads = [pltpu.make_async_copy(w_hbm.at[dx], w_ref.at[dx], w_sem.at[dx]) for dx in range(3)]
     load_v.start()
-    load_w.start()
+    loads[1].start()
+    loads[0].start(priority=1)
+    loads[2].start(priority=1)
+    planes, ny, nz, nc = v_ref.shape
     at_z = lax.axis_index("gz")
     load_v.wait()
     for p in range(v_ref.shape[0]):
         shifted_copies(v_ref[p], shift_ref, p, 1)
         column_ref[p] = edge_columns(v_ref[p], flat_ref, at_z)
-    load_w.wait()
-
-
-def pack_kernel(r_ref, w_ref, own_ref, column_ref, out_ref, h_ref, shift_ref, flat_ref, pair_ref):
+    loads[1].wait()
+    step = ny // 2
+    for p in range(planes):
+        for first in range(0, ny, step):
+            begin = (p * ny + first) * nz
+            rhs = w_ref[1].reshape(9 * nc, w_ref.shape[4])
+            sums = jnp.dot(windows(shift_ref, p, first, step), rhs, preferred_element_type=F32)
+            sum_ref[begin : begin + step * nz] = sums
+    loads[0].wait()
+    loads[2].wait()
+
+
+def pack_kernel(r_ref, w_ref, own_ref, column_ref, sum_ref, out_ref, h_ref, shift_ref, flat_ref, pair_ref):
     at_x, at_y, at_z = (lax.axis_index(axis) for axis in GROUP)
     planes, ny, nz, nc = r_ref.shape
     filters = w_ref.shape[4]
@@ -140,14 +152,17 @@
     put_edges(2 * mine, shift_ref, 0, edge_columns(plane, flat_ref, at_z))
     for p in range(planes):
         put_edges(at_x + p, own_ref, p, column_ref[p])
-    step = 8
+    step = 16
     for first in range(0, ny, step):
-        lhs = jnp.concatenate([windows(own_ref, source, first, step) for source in range(planes)], axis=1)
-        halo = windows(shift_ref, 0, first, step)
-        sums = jnp.dot(lhs, w_ref[pl.ds(at_x, planes)].reshape(planes * 9 * nc, filters), preferred_element_type=F32)
-        sums += jnp.dot(halo, w_ref[2 * mine].reshape(9 * nc, filters), preferred_element_type=F32)
-        rest = w_ref[pl.ds(mine, planes)].reshape(planes * 9 * nc, filters)
-        h_ref[first * nz : (first + step) * nz] = jnp.maximum(sums, jnp.dot(lhs, rest, preferred_element_type=F32))
+        count = step * nz
+        near = w_ref[2 * mine].reshape(9 * nc, filters)
+        far = w_ref[2 * at_x].reshape(9 * nc, filters)
+        inner = sum_ref[pl.ds(pl.multiple_of(mine * rows + first * nz, 8), count)]
+        inner += jnp.dot(windows(shift_ref, 0, first, step), near, preferred_element_type=F32)
+        inner += jnp.dot(windows(own_ref, at_x, first, step), far, preferred_element_type=F32)
+        outer = sum_ref[pl.ds(pl.multiple_of(at_x * rows + first * nz, 8), count)]
+        outer += jnp.dot(windows(own_ref, mine, first, step), near, preferred_element_type=F32)
+        h_ref[first * nz : first * nz + count] = jnp.maximum(inner, outer)
 
     def row(y):
         return h_ref[y * nz : (y + 1) * nz]
@@ -272,20 +287,21 @@
     cost = functools.partial(pl.CostEstimate, transcendentals=0)
     rows = ny * nz
     theirs = swap(volume, 4)
-    moved, columns, kernel4 = pl.pallas_call(
+    moved, columns, sums, kernel4 = pl.pallas_call(
         prepare_kernel,
         out_shape=(
             jax.ShapeDtypeStruct((3, planes, ny + 2, nz, nc), BF),
             jax.ShapeDtypeStruct((planes, ny, 2 * nc), BF),
+            jax.ShapeDtypeStruct((planes * rows, f4), F32),
             jax.ShapeDtypeStruct(conv4_weight.shape, BF),
         ),
         in_specs=[HBM, HBM],
-        out_specs=(VMEM, VMEM, VMEM),
+        out_specs=(VMEM,) * 4,
         scratch_shapes=[
             pltpu.VMEM(volume.shape, BF),
             pltpu.VMEM((rows, nc), F32),
             pltpu.SemaphoreType.DMA,
-            pltpu.SemaphoreType.DMA,
+            pltpu.SemaphoreType.DMA((3,)),
         ],
         cost_estimate=cost(flops=20 * planes * rows * nc, bytes_accessed=54 * nc * f4),
         compiler_params=PARAMS,
@@ -295,7 +311,7 @@
     pack = pl.pallas_call(
         pack_kernel,
         out_shape=jax.ShapeDtypeStruct((packed, f4), BF),
-        in_specs=[VMEM] * 4,
+        in_specs=[VMEM] * 5,
         out_specs=VMEM,
         scratch_shapes=[
             pltpu.VMEM((rows, f4), F32),
@@ -303,10 +319,10 @@
             pltpu.VMEM((rows, nc), F32),
             pltpu.VMEM((f4 // 128, rows // 2, 128), F32),
         ],
-        cost_estimate=cost(flops=5 * 2 * rows * 9 * nc * f4, bytes_accessed=54 * nc * f4),
+        cost_estimate=cost(flops=3 * 2 * rows * 9 * nc * f4, bytes_accessed=54 * nc * f4),
         compiler_params=PARAMS,
         name="conv4_pool_pack",
-    )(theirs, kernel4, moved, columns)
+    )(theirs, kernel4, moved, columns, sums)
     by_y = swap(pack, 2)
     by_z = swap(pack, 1)
     by_both = swap(pack, 3)

time: 15 us -> 14.9 us (level)
    pallas_call x1, Pallas kernels: 0.99 us -> 0.72 us  [pair_body(): pl.pallas_call(pack_kernel, out_shape=jax.ShapeDtypeStruct((packed, f4),...]
    pallas_call x1, Pallas kernels: 1.57 us -> 1.81 us  [pair_body(): pl.pallas_call(prepare_kernel, out_shape=(jax.ShapeDtypeStruct((3, planes...]
  transfers between devices with their start and end apart: 5 -> 5, of which waited for: 4 -> 4; matrix products, arithmetic and copies ran while one was open for 0% -> 0% of each run, Pallas kernels for 11% -> 12%
where the time goes in v6:
time: 14.9 us; the launch traced here: 14.8 us
  waiting for transfers between devices  5.71 us (38%)
  starting transfers between devices  4.69 us (31%)
  Pallas kernels  4.34 us (29%)
    ppermute x5, waiting for transfers between devices, swap(): return lax.ppermute(x, GROUP, [(i, i ^ flips) for i in range(8)])  5.71 us
    ppermute x5, starting transfers between devices, swap(): return lax.ppermute(x, GROUP, [(i, i ^ flips) for i in range(8)])  4.69 us
    pallas_call x1, Pallas kernels, pair_body(): pl.pallas_call(prepare_kernel, out_shape=(jax.ShapeDtypeStruct((3, planes...  1.81 us
    pallas_call x1, Pallas kernels, pair_body(): pl.pallas_call(functools.partial(finish_kernel, ny=ny, nz=nz, planes=plan...  1.17 us
    pallas_call x1, Pallas kernels, pair_body(): pl.pallas_call(pack_kernel, out_shape=jax.ShapeDtypeStruct((packed, f4),...  0.72 us
    pallas_call x1, Pallas kernels, pair_body(): pl.pallas_call(add_kernel, out_shape=jax.ShapeDtypeStruct((gy * gz, f5),...  0.64 us
  transfers between devices with their start and end apart: 5, of which 4 were waited for; matrix products, arithmetic and copies ran while one was open for 0% of the time, Pallas kernels for 12%

profile of v6, /device:TPU:0, one launch (start us, length us, event | category | flops | bytes accessed | tf_op | source)
XLA Modules:
  0.0 14.8 jit_solution(3762315625260437501)
XLA Ops:
  0.0 0.5 %collective-permute-start = (bf16[2,16,16,128]{3,2,1,0:T(8,128)(2,1)}, bf16[2,16,16,128]{3,2,1,0:T(8,128)(2,1)S(1)}, u32[]{:S(2)}, u32[]{:S(2)}) collective-permute-start(bf16[2,16,16,128]{3,2,1,0:T(8,128)(2,1)} %v_hbm.1), channel_id=1, source_target_pairs={{0,4},{1,5},{2,6},{3,7},{4,0},{5,1},{6,2},{7,3},{8,12},{9,13},{10,... | collective-permute-start | bytes 393224 | tf_op jit(solution)/shard_map/ppermute | solution.py:285
  0.5 1.8 %prepare.1 = (bf16[3,2,18,16,128]{4,3,2,1,0:T(8,128)(2,1)S(1)}, bf16[2,16,256]{2,1,0:T(8,128)(2,1)S(1)}, f32[512,256]{1,0:T(8,128)S(1)}, bf16[3,3,3,128,256]{4,3,2,1,0:T(8,128)(2,1)S(1)}) custom-call(bf16[2,16,16,128]{3,2,1,0:T(8,128)(2,1)} %v_hbm.1, bf16[3,3,3,128,256]{4,3,2,1,0:T(8,128)(2,1)} %w_hbm.1), custom_call_target="tpu_custom_call" | custom-call | flops 1310720 | bytes 1769472 | tf_op jit(solution)/shard_map/prepare/pallas_call | solution.py:290
  2.3 0.0 copy-start
  2.3 0.0 collective-permute-done.r_ref
  2.3 0.7 %conv4_pool_pack.1.q0 = bf16[160,256]{1,0:T(8,128)(2,1)S(1)} custom-call(bf16[2,16,16,128]{3,2,1,0:T(8,128)(2,1)S(1)} %collective-permute-done.r_ref, bf16[3,3,3,128,256]{4,3,2,1,0:T(8,128)(2,1)S(1)} %get-tuple-element.11.w_ref.w4_ref, bf16[3,2,18,16,128]{4,3,2,1,0:T(8,128)(2,1)S(1)} %get-tuple-element.12.own_ref, ...), custom_call_target="tpu_custom_call" | custom-call | flops 452984832 | bytes 1769472 | tf_op jit(solution)/shard_map/conv4_pool_pack/pallas_call | solution.py:311
  3.0 3.5 %collective-permute-start.3 = (bf16[160,256]{1,0:T(8,128)(2,1)S(1)}, bf16[160,256]{1,0:T(8,128)(2,1)S(1)}, u32[]{:S(2)}, u32[]{:S(2)}) collective-permute-start(bf16[160,256]{1,0:T(8,128)(2,1)S(1)} %conv4_pool_pack.1.q0), channel_id=1, source_target_pairs={{0,3},{1,2},{2,1},{3,0},{4,7},{5,6},{6,5},{7,4},{8,11},{9,10},{10,... | collective-permute-start | bytes 245768 | tf_op jit(solution)/shard_map/ppermute | solution.py:285
  6.5 0.5 %collective-permute-start.2 = (bf16[160,256]{1,0:T(8,128)(2,1)S(1)}, bf16[160,256]{1,0:T(8,128)(2,1)S(1)}, u32[]{:S(2)}, u32[]{:S(2)}) collective-permute-start(bf16[160,256]{1,0:T(8,128)(2,1)S(1)} %conv4_pool_pack.1.q0), channel_id=1, source_target_pairs={{0,1},{1,0},{2,3},{3,2},{4,5},{5,4},{6,7},{7,6},{8,9},{9,8},{10,11... | collective-permute-start | bytes 245768 | tf_op jit(solution)/shard_map/ppermute | solution.py:285
  7.0 0.1 collective-permute-start.1
  7.2 2.5 %collective-permute-done.3.q3 = bf16[160,256]{1,0:T(8,128)(2,1)S(1)} collective-permute-done((bf16[160,256]{1,0:T(8,128)(2,1)S(1)}, bf16[160,256]{1,0:T(8,128)(2,1)S(1)}, u32[]{:S(2)}, u32[]{:S(2)}) %collective-permute-start.3) | collective-permute-done | bytes 81952 | tf_op jit(solution)/shard_map/ppermute | solution.py:285
  9.7 1.7 %collective-permute-done.2.q2 = bf16[160,256]{1,0:T(8,128)(2,1)S(1)} collective-permute-done((bf16[160,256]{1,0:T(8,128)(2,1)S(1)}, bf16[160,256]{1,0:T(8,128)(2,1)S(1)}, u32[]{:S(2)}, u32[]{:S(2)}) %collective-permute-start.2) | collective-permute-done | bytes 81952 | tf_op jit(solution)/shard_map/ppermute | solution.py:285
  11.4 0.2 %collective-permute-done.1.q1 = bf16[160,256]{1,0:T(8,128)(2,1)S(1)} collective-permute-done((bf16[160,256]{1,0:T(8,128)(2,1)S(1)}, bf16[160,256]{1,0:T(8,128)(2,1)S(1)}, u32[]{:S(2)}, u32[]{:S(2)}) %collective-permute-start.1) | collective-permute-done | bytes 81952 | tf_op jit(solution)/shard_map/ppermute | solution.py:285
  11.6 0.0 copy-done
  11.6 1.2 %finish_and_conv5.1 = (f32[256,128]{1,0:T(8,128)S(1)}, bf16[256,128]{1,0:T(8,128)(2,1)S(1)}) custom-call(bf16[160,256]{1,0:T(8,128)(2,1)S(1)} %conv4_pool_pack.1.q0, bf16[160,256]{1,0:T(8,128)(2,1)S(1)} %collective-permute-done.1.q1, bf16[160,256]{1,0:T(8,128)(2,1)S(1)} %collective-permute-done.2.q2, bf16[160,256]{1,0:T(8,128)(2,1)S(1)} %collective-permute-done.3.q3, ...), custom_call_target="tpu_custom_call" | custom-call | flops 301989888 | bytes 1179648 | tf_op jit(solution)/shard_map/finish_and_conv5/pallas_call | solution.py:330
  12.8 0.1 collective-permute-start.4
  12.9 1.2 %collective-permute-done.4.other_ref = bf16[256,128]{1,0:T(8,128)(2,1)S(1)} collective-permute-done((bf16[256,128]{1,0:T(8,128)(2,1)S(1)}, bf16[256,128]{1,0:T(8,128)(2,1)S(1)}, u32[]{:S(2)}, u32[]{:S(2)}) %collective-permute-start.4) | collective-permute-done | bytes 65568 | tf_op jit(solution)/shard_map/ppermute | solution.py:285
  14.1 0.6 %add_planes.1 = bf16[256,128]{1,0:T(8,128)(2,1)} custom-call(f32[256,128]{1,0:T(8,128)S(1)} %get-tuple-element.15.own_ref, bf16[256,128]{1,0:T(8,128)(2,1)S(1)} %collective-permute-done.4.other_ref), custom_call_target="tpu_custom_call" | custom-call | tf_op jit(solution)/shard_map/add_planes/pallas_call | solution.py:347
Async XLA Ops:
  0.0 2.3 %collective-permute-start = (bf16[2,16,16,128]{3,2,1,0:T(8,128)(2,1)}, bf16[2,16,16,128]{3,2,1,0:T(8,128)(2,1)S(1)}, u32[]{:S(2)}, u32[]{:S(2)}) collective-permute-start(bf16[2,16,16,128]{3,2,1,0:T(8,128)(2,1)} %v_hbm.1), channel_id=1, source_target_pairs={{0,4},{1,5},{2,6},{3,7},{4,0},{5,1},{6,2},{7,3},{8,12},{9,13},{10,... | collective-permute-start | bytes 393224 | tf_op jit(solution)/shard_map/ppermute | solution.py:285
  2.3 9.4 %copy-start = (bf16[3,3,3,256,128]{4,3,2,1,0:T(8,128)(2,1)S(1)}, bf16[3,3,3,256,128]{4,3,2,1,0:T(8,128)(2,1)}, u32[]{:S(2)}) copy-start(bf16[3,3,3,256,128]{4,3,2,1,0:T(8,128)(2,1)} %w_ref.1) | copy-start | bytes 5308420
  3.0 6.7 %collective-permute-start.3 = (bf16[160,256]{1,0:T(8,128)(2,1)S(1)}, bf16[160,256]{1,0:T(8,128)(2,1)S(1)}, u32[]{:S(2)}, u32[]{:S(2)}) collective-permute-start(bf16[160,256]{1,0:T(8,128)(2,1)S(1)} %conv4_pool_pack.1.q0), channel_id=1, source_target_pairs={{0,3},{1,2},{2,1},{3,0},{4,7},{5,6},{6,5},{7,4},{8,11},{9,10},{10,... | collective-permute-start | bytes 245768 | tf_op jit(solution)/shard_map/ppermute | solution.py:285
  6.5 4.9 %collective-permute-start.2 = (bf16[160,256]{1,0:T(8,128)(2,1)S(1)}, bf16[160,256]{1,0:T(8,128)(2,1)S(1)}, u32[]{:S(2)}, u32[]{:S(2)}) collective-permute-start(bf16[160,256]{1,0:T(8,128)(2,1)S(1)} %conv4_pool_pack.1.q0), channel_id=1, source_target_pairs={{0,1},{1,0},{2,3},{3,2},{4,5},{5,4},{6,7},{7,6},{8,9},{9,8},{10,11... | collective-permute-start | bytes 245768 | tf_op jit(solution)/shard_map/ppermute | solution.py:285
  7.0 4.6 %collective-permute-start.1 = (bf16[160,256]{1,0:T(8,128)(2,1)S(1)}, bf16[160,256]{1,0:T(8,128)(2,1)S(1)}, u32[]{:S(2)}, u32[]{:S(2)}) collective-permute-start(bf16[160,256]{1,0:T(8,128)(2,1)S(1)} %conv4_pool_pack.1.q0), channel_id=1, source_target_pairs={{0,2},{1,3},{2,0},{3,1},{4,6},{5,7},{6,4},{7,5},{8,10},{9,11},{10,... | collective-permute-start | bytes 245768 | tf_op jit(solution)/shard_map/ppermute | solution.py:285
  12.8 1.3 %collective-permute-start.4 = (bf16[256,128]{1,0:T(8,128)(2,1)S(1)}, bf16[256,128]{1,0:T(8,128)(2,1)S(1)}, u32[]{:S(2)}, u32[]{:S(2)}) collective-permute-start(bf16[256,128]{1,0:T(8,128)(2,1)S(1)} %get-tuple-element.16), channel_id=1, source_target_pairs={{0,4},{1,5},{2,6},{3,7},{4,0},{5,1},{6,2},{7,3},{8,12},{9,13},{10,... | collective-permute-start | bytes 196616 | tf_op jit(solution)/shard_map/ppermute | solution.py:285

commit v7 on v6

--- a/solution.py
+++ b/solution.py
@@ -282,7 +282,7 @@
     f4, f5 = conv4_weight.shape[4], conv5_weight.shape[4]
 
     def swap(x, flips):
-        return lax.ppermute(x, GROUP, [(i, i ^ flips) for i in range(8)])
+        return lax.ppermute(x, GROUP, [(i, i ^ flips) for i in range(lax.axis_size(GROUP))])
 
     cost = functools.partial(pl.CostEstimate, transcendentals=0)
     rows = ny * nz

time: 14.9 us -> 14.9 us (level)
  no operation moved by 1% of the time
where the time goes in v7:
time: 14.9 us; the launch traced here: 14.8 us
  waiting for transfers between devices  5.71 us (38%)
  starting transfers between devices  4.69 us (31%)
  Pallas kernels  4.34 us (29%)
    ppermute x5, waiting for transfers between devices, swap(): lax.ppermute(x, GROUP, [(i, i ^ flips) for i in range(lax.axis_size(GROUP...  5.71 us
    ppermute x5, starting transfers between devices, swap(): lax.ppermute(x, GROUP, [(i, i ^ flips) for i in range(lax.axis_size(GROUP...  4.69 us
    pallas_call x1, Pallas kernels, pair_body(): pl.pallas_call(prepare_kernel, out_shape=(jax.ShapeDtypeStruct((3, planes...  1.81 us
    pallas_call x1, Pallas kernels, pair_body(): pl.pallas_call(functools.partial(finish_kernel, ny=ny, nz=nz, planes=plan...  1.17 us
    pallas_call x1, Pallas kernels, pair_body(): pl.pallas_call(pack_kernel, out_shape=jax.ShapeDtypeStruct((packed, f4),...  0.72 us
    pallas_call x1, Pallas kernels, pair_body(): pl.pallas_call(add_kernel, out_shape=jax.ShapeDtypeStruct((gy * gz, f5),...  0.64 us
  transfers between devices with their start and end apart: 5, of which 4 were waited for; matrix products, arithmetic and copies ran while one was open for 0% of the time, Pallas kernels for 12%

profile of v7, /device:TPU:0, one launch (start us, length us, event | category | flops | bytes accessed | tf_op | source)
XLA Modules:
  0.0 14.8 jit_solution(3762315625260437501)
XLA Ops:
  0.0 0.5 %collective-permute-start = (bf16[2,16,16,128]{3,2,1,0:T(8,128)(2,1)}, bf16[2,16,16,128]{3,2,1,0:T(8,128)(2,1)S(1)}, u32[]{:S(2)}, u32[]{:S(2)}) collective-permute-start(bf16[2,16,16,128]{3,2,1,0:T(8,128)(2,1)} %v_hbm.1), channel_id=1, source_target_pairs={{0,4},{1,5},{2,6},{3,7},{4,0},{5,1},{6,2},{7,3},{8,12},{9,13},{10,... | collective-permute-start | bytes 393224 | tf_op jit(solution)/shard_map/ppermute | solution.py:285
  0.5 1.8 %prepare.1 = (bf16[3,2,18,16,128]{4,3,2,1,0:T(8,128)(2,1)S(1)}, bf16[2,16,256]{2,1,0:T(8,128)(2,1)S(1)}, f32[512,256]{1,0:T(8,128)S(1)}, bf16[3,3,3,128,256]{4,3,2,1,0:T(8,128)(2,1)S(1)}) custom-call(bf16[2,16,16,128]{3,2,1,0:T(8,128)(2,1)} %v_hbm.1, bf16[3,3,3,128,256]{4,3,2,1,0:T(8,128)(2,1)} %w_hbm.1), custom_call_target="tpu_custom_call" | custom-call | flops 1310720 | bytes 1769472 | tf_op jit(solution)/shard_map/prepare/pallas_call | solution.py:290
  2.3 0.0 copy-start
  2.3 0.0 collective-permute-done.r_ref
  2.3 0.7 %conv4_pool_pack.1.q0 = bf16[160,256]{1,0:T(8,128)(2,1)S(1)} custom-call(bf16[2,16,16,128]{3,2,1,0:T(8,128)(2,1)S(1)} %collective-permute-done.r_ref, bf16[3,3,3,128,256]{4,3,2,1,0:T(8,128)(2,1)S(1)} %get-tuple-element.11.w_ref.w4_ref, bf16[3,2,18,16,128]{4,3,2,1,0:T(8,128)(2,1)S(1)} %get-tuple-element.12.own_ref, ...), custom_call_target="tpu_custom_call" | custom-call | flops 452984832 | bytes 1769472 | tf_op jit(solution)/shard_map/conv4_pool_pack/pallas_call | solution.py:311
  3.0 3.5 %collective-permute-start.3 = (bf16[160,256]{1,0:T(8,128)(2,1)S(1)}, bf16[160,256]{1,0:T(8,128)(2,1)S(1)}, u32[]{:S(2)}, u32[]{:S(2)}) collective-permute-start(bf16[160,256]{1,0:T(8,128)(2,1)S(1)} %conv4_pool_pack.1.q0), channel_id=1, source_target_pairs={{0,3},{1,2},{2,1},{3,0},{4,7},{5,6},{6,5},{7,4},{8,11},{9,10},{10,... | collective-permute-start | bytes 245768 | tf_op jit(solution)/shard_map/ppermute | solution.py:285
  6.5 0.5 %collective-permute-start.2 = (bf16[160,256]{1,0:T(8,128)(2,1)S(1)}, bf16[160,256]{1,0:T(8,128)(2,1)S(1)}, u32[]{:S(2)}, u32[]{:S(2)}) collective-permute-start(bf16[160,256]{1,0:T(8,128)(2,1)S(1)} %conv4_pool_pack.1.q0), channel_id=1, source_target_pairs={{0,1},{1,0},{2,3},{3,2},{4,5},{5,4},{6,7},{7,6},{8,9},{9,8},{10,11... | collective-permute-start | bytes 245768 | tf_op jit(solution)/shard_map/ppermute | solution.py:285
  7.0 0.1 collective-permute-start.1
  7.2 2.5 %collective-permute-done.3.q3 = bf16[160,256]{1,0:T(8,128)(2,1)S(1)} collective-permute-done((bf16[160,256]{1,0:T(8,128)(2,1)S(1)}, bf16[160,256]{1,0:T(8,128)(2,1)S(1)}, u32[]{:S(2)}, u32[]{:S(2)}) %collective-permute-start.3) | collective-permute-done | bytes 81952 | tf_op jit(solution)/shard_map/ppermute | solution.py:285
  9.7 1.7 %collective-permute-done.2.q2 = bf16[160,256]{1,0:T(8,128)(2,1)S(1)} collective-permute-done((bf16[160,256]{1,0:T(8,128)(2,1)S(1)}, bf16[160,256]{1,0:T(8,128)(2,1)S(1)}, u32[]{:S(2)}, u32[]{:S(2)}) %collective-permute-start.2) | collective-permute-done | bytes 81952 | tf_op jit(solution)/shard_map/ppermute | solution.py:285
  11.4 0.2 %collective-permute-done.1.q1 = bf16[160,256]{1,0:T(8,128)(2,1)S(1)} collective-permute-done((bf16[160,256]{1,0:T(8,128)(2,1)S(1)}, bf16[160,256]{1,0:T(8,128)(2,1)S(1)}, u32[]{:S(2)}, u32[]{:S(2)}) %collective-permute-start.1) | collective-permute-done | bytes 81952 | tf_op jit(solution)/shard_map/ppermute | solution.py:285
  11.6 0.0 copy-done
  11.6 1.2 %finish_and_conv5.1 = (f32[256,128]{1,0:T(8,128)S(1)}, bf16[256,128]{1,0:T(8,128)(2,1)S(1)}) custom-call(bf16[160,256]{1,0:T(8,128)(2,1)S(1)} %conv4_pool_pack.1.q0, bf16[160,256]{1,0:T(8,128)(2,1)S(1)} %collective-permute-done.1.q1, bf16[160,256]{1,0:T(8,128)(2,1)S(1)} %collective-permute-done.2.q2, bf16[160,256]{1,0:T(8,128)(2,1)S(1)} %collective-permute-done.3.q3, ...), custom_call_target="tpu_custom_call" | custom-call | flops 301989888 | bytes 1179648 | tf_op jit(solution)/shard_map/finish_and_conv5/pallas_call | solution.py:330
  12.8 0.1 collective-permute-start.4
  12.9 1.2 %collective-permute-done.4.other_ref = bf16[256,128]{1,0:T(8,128)(2,1)S(1)} collective-permute-done((bf16[256,128]{1,0:T(8,128)(2,1)S(1)}, bf16[256,128]{1,0:T(8,128)(2,1)S(1)}, u32[]{:S(2)}, u32[]{:S(2)}) %collective-permute-start.4) | collective-permute-done | bytes 65568 | tf_op jit(solution)/shard_map/ppermute | solution.py:285
  14.1 0.6 %add_planes.1 = bf16[256,128]{1,0:T(8,128)(2,1)} custom-call(f32[256,128]{1,0:T(8,128)S(1)} %get-tuple-element.15.own_ref, bf16[256,128]{1,0:T(8,128)(2,1)S(1)} %collective-permute-done.4.other_ref), custom_call_target="tpu_custom_call" | custom-call | tf_op jit(solution)/shard_map/add_planes/pallas_call | solution.py:347
Async XLA Ops:
  0.0 2.3 %collective-permute-start = (bf16[2,16,16,128]{3,2,1,0:T(8,128)(2,1)}, bf16[2,16,16,128]{3,2,1,0:T(8,128)(2,1)S(1)}, u32[]{:S(2)}, u32[]{:S(2)}) collective-permute-start(bf16[2,16,16,128]{3,2,1,0:T(8,128)(2,1)} %v_hbm.1), channel_id=1, source_target_pairs={{0,4},{1,5},{2,6},{3,7},{4,0},{5,1},{6,2},{7,3},{8,12},{9,13},{10,... | collective-permute-start | bytes 393224 | tf_op jit(solution)/shard_map/ppermute | solution.py:285
  2.3 9.4 %copy-start = (bf16[3,3,3,256,128]{4,3,2,1,0:T(8,128)(2,1)S(1)}, bf16[3,3,3,256,128]{4,3,2,1,0:T(8,128)(2,1)}, u32[]{:S(2)}) copy-start(bf16[3,3,3,256,128]{4,3,2,1,0:T(8,128)(2,1)} %w_ref.1) | copy-start | bytes 5308420
  3.0 6.7 %collective-permute-start.3 = (bf16[160,256]{1,0:T(8,128)(2,1)S(1)}, bf16[160,256]{1,0:T(8,128)(2,1)S(1)}, u32[]{:S(2)}, u32[]{:S(2)}) collective-permute-start(bf16[160,256]{1,0:T(8,128)(2,1)S(1)} %conv4_pool_pack.1.q0), channel_id=1, source_target_pairs={{0,3},{1,2},{2,1},{3,0},{4,7},{5,6},{6,5},{7,4},{8,11},{9,10},{10,... | collective-permute-start | bytes 245768 | tf_op jit(solution)/shard_map/ppermute | solution.py:285
  6.5 4.9 %collective-permute-start.2 = (bf16[160,256]{1,0:T(8,128)(2,1)S(1)}, bf16[160,256]{1,0:T(8,128)(2,1)S(1)}, u32[]{:S(2)}, u32[]{:S(2)}) collective-permute-start(bf16[160,256]{1,0:T(8,128)(2,1)S(1)} %conv4_pool_pack.1.q0), channel_id=1, source_target_pairs={{0,1},{1,0},{2,3},{3,2},{4,5},{5,4},{6,7},{7,6},{8,9},{9,8},{10,11... | collective-permute-start | bytes 245768 | tf_op jit(solution)/shard_map/ppermute | solution.py:285
  7.0 4.6 %collective-permute-start.1 = (bf16[160,256]{1,0:T(8,128)(2,1)S(1)}, bf16[160,256]{1,0:T(8,128)(2,1)S(1)}, u32[]{:S(2)}, u32[]{:S(2)}) collective-permute-start(bf16[160,256]{1,0:T(8,128)(2,1)S(1)} %conv4_pool_pack.1.q0), channel_id=1, source_target_pairs={{0,2},{1,3},{2,0},{3,1},{4,6},{5,7},{6,4},{7,5},{8,10},{9,11},{10,... | collective-permute-start | bytes 245768 | tf_op jit(solution)/shard_map/ppermute | solution.py:285
  12.8 1.3 %collective-permute-start.4 = (bf16[256,128]{1,0:T(8,128)(2,1)S(1)}, bf16[256,128]{1,0:T(8,128)(2,1)S(1)}, u32[]{:S(2)}, u32[]{:S(2)}) collective-permute-start(bf16[256,128]{1,0:T(8,128)(2,1)S(1)} %get-tuple-element.16), channel_id=1, source_target_pairs={{0,4},{1,5},{2,6},{3,7},{4,0},{5,1},{6,2},{7,3},{8,12},{9,13},{10,... | collective-permute-start | bytes 196616 | tf_op jit(solution)/shard_map/ppermute | solution.py:285
